TPU v7x, 256 devices: a whole 4x4x8 slice. The times are simulated.
256 devices in a mesh: ed: 16 (over z, core), ep: 16 (over y, x).
Axes of the slice: x: 4, y: 4, z: 8, core: 2. Of those that a mesh axis runs over, the one named last changes fastest.
Arguments:
- out_grad: bfloat16 [32768, 3584], P(('ed', 'ep')), may hold values from -4.1 to 4.1
- routes: int32 [32768, 2], P(('ed', 'ep')), may hold values from 0 to 15, all different within a row; in each aligned block of 128 rows (0 to 127, 128 to 255, ...) at most 32 rows name the same one
- gates: bfloat16 [32768, 2], P(('ed', 'ep')), may hold values from 0.049804688 to 0.59765625
- pre_acts: bfloat16 [16, 16, 16, 32, 2048], P('ed', 'ep'), may hold values from -6 to 6
- down_weight: bfloat16 [16, 1024, 3584], P('ep'), may hold values from -0.1875 to 0.1875
- history: float32 [16, 16, 16], P('ed', 'ep'), may hold values from 4 to 32
Outputs:
- pre_grad: bfloat16 [16, 16, 16, 32, 2048], P('ed', 'ep')
- wgrad: float32 [16, 3584, 1024], P('ep', 'ed')
- new_history: float32 [16, 16], P('ep')
- gate_grad: float32 [32768, 2], P(('ed', 'ep'))
Inputs may be any that keep to these rules, and one draw needn't show every extreme that they name: `routes`: each token names 2 different experts; among the 128 rows of one device no expert is named more than 32 times, and in some device's rows one expert is named exactly 32 times.
All inputs are finite; a program needn't handle non-finite values.
Results may differ from a plain program's by a relative error of at most 0.025.
Values may be sent and summed in bfloat16 or wider, within the bound.
No kernel may reach another device: no remote copies, remote signals or barrier semaphores. Data moves between devices by JAX's collectives and lax.ppermute only.
A program may use at most 128 MiB of HBM per device.

v0:
```python
import jax
import jax.numpy as jnp
from jax import lax
from jax.sharding import PartitionSpec as P


def split_pre(pre_block, width_ff):
    gate_pre = pre_block[:, :width_ff].astype(jnp.float32)
    up_pre = pre_block[:, width_ff:].astype(jnp.float32)
    return (gate_pre, up_pre, jax.nn.sigmoid(gate_pre))


def body(out_grad, routes, gates, pre_acts, down_weight, history):
    tok_rows, top = routes.shape
    width = out_grad.shape[1]
    local = down_weight.shape[0]
    width_ff = down_weight.shape[1]
    n_src = pre_acts.shape[2]
    cap = pre_acts.shape[3]
    n_ep = lax.axis_size("ep")
    n_replicas = lax.axis_size("ed")
    experts = local * n_ep
    flat = routes.reshape(-1)
    hits = (flat[:, None] == jnp.arange(experts, dtype=jnp.int32)[None, :]).astype(jnp.int32)
    before = jnp.cumsum(hits, axis=0) - hits
    slot = jnp.sum(before * hits, axis=1)
    target = flat * cap + slot
    owner = jnp.arange(tok_rows * top, dtype=jnp.int32) // top
    table = jnp.zeros((experts * cap,), jnp.int32).at[target].set(owner + 1)
    picked = out_grad[jnp.maximum(table - 1, 0)]
    send_rows = jnp.where((table > 0)[:, None], picked, jnp.zeros_like(picked))
    send_gate = jnp.zeros((experts * cap,), jnp.bfloat16).at[target].set(gates.reshape(-1))
    arrived, arrived_gate = (
        lax.all_to_all(
            send_rows.reshape(n_ep, local * cap, width),
            "ep",
            split_axis=0,
            concat_axis=0,
            tiled=True,
        ),
        lax.all_to_all(
            send_gate.reshape(n_ep, local * cap), "ep", split_axis=0, concat_axis=0, tiled=True
        ),
    )
    arrived = (
        arrived.reshape(n_ep, local, cap, width)
        .transpose(1, 0, 2, 3)
        .reshape(local, n_ep * cap, width)
    )
    arrived_gate = (
        arrived_gate.reshape(n_ep, local, cap)
        .transpose(1, 0, 2)
        .reshape(local, n_ep * cap)
        .astype(jnp.float32)
    )
    merged = lax.pmax(history, "ed")[0]
    ref_amax = jnp.max(merged, axis=1)
    scale = 1.0 / ref_amax
    rows = arrived[0]
    gate_row = arrived_gate[0][:, None]
    weight = down_weight[0]
    pre_block = pre_acts[0, 0].reshape(n_src * cap, 2 * width_ff)
    gate_pre, up_pre, sigma = split_pre(pre_block, width_ff)
    act = (gate_pre * sigma * up_pre).astype(jnp.bfloat16)
    weighted = (gate_row * act.astype(jnp.float32)).astype(jnp.bfloat16)
    raw = jnp.einsum("rd,hd->rh", rows, weight, preferred_element_type=jnp.float32)
    score = jnp.sum(act.astype(jnp.float32) * raw, axis=1)
    grad_act = gate_row * raw
    grad_gate = grad_act * up_pre * sigma * (1.0 + gate_pre * (1.0 - sigma))
    grad_up = grad_act * gate_pre * sigma
    grads_pre = [
        jnp.concatenate([grad_gate, grad_up], axis=1)
        .astype(jnp.bfloat16)
        .reshape(n_src, cap, 2 * width_ff)
    ]
    scores = [score.reshape(n_ep, cap)]
    factor = scale[0]

    def term(start, count, rows=rows, weighted=weighted, factor=factor):
        return factor * jnp.einsum("rd,rh->dh", rows, weighted, preferred_element_type=jnp.float32)

    shard = lax.psum_scatter(
        term(jnp.int32(0), width // n_replicas * lax.axis_size("ed")).astype(jnp.bfloat16),
        "ed",
        scatter_dimension=0,
        tiled=True,
    ).astype(jnp.float32)
    shards = [shard]
    wgrad = jnp.stack(shards)
    peak = lax.pmax(jnp.max(jnp.abs(wgrad), axis=(1, 2)), "ed")
    new_amax = peak * ref_amax
    new_history = jnp.concatenate([merged[:, 1:], new_amax[:, None]], axis=1)
    pre_grad = jnp.stack(grads_pre)[None]
    outgoing = jnp.stack(scores).transpose(1, 0, 2).reshape(n_ep, local * cap)
    returned = lax.all_to_all(outgoing, "ep", split_axis=0, concat_axis=0, tiled=True)
    gate_grad = returned.reshape(-1)[target].reshape(tok_rows, top)
    return (pre_grad, wgrad, new_history, gate_grad)


def solution(mesh):
    placed = (
        P(("ed", "ep"), None),
        P(("ed", "ep"), None),
        P(("ed", "ep"), None),
        P("ed", "ep", None, None, None),
        P("ep", None, None),
        P("ed", "ep", None),
    )
    return jax.shard_map(
        body,
        mesh=mesh,
        in_specs=placed,
        out_specs=(
            P("ed", "ep", None, None, None),
            P("ep", "ed", None),
            P("ep", None),
            P(("ed", "ep"), None),
        ),
        check_vma=False,
    )
```

profile of v0, /device:TPU:1, one launch (start us, length us, event | category | flops | bytes accessed | tf_op | source)
XLA Modules:
  0.0 207.2 jit_solution(18365370312476439625)
XLA Ops:
  7.2 0.0 copy-start
  7.2 0.8 broadcast_multiply_fusion
  7.9 0.8 copy.17
  8.7 0.1 eq.29
  8.9 0.1 eq.25
  9.0 0.8 copy.20
  9.8 0.1 reshape.149
  9.9 0.1 copy.16
  10.1 0.1 mul.71
  10.2 0.6 reduce-window.6
  10.8 0.2 slice_reduce_fusion
  11.0 0.1 fusion.19
  11.1 2.2 %scatter_custom_fusion = bf16[512]{0:T(512)(128)(2,1)S(1)} fusion(s32[256]{0:T(256)S(1)} %bitcast.45, bf16[256]{0:T(256)(128)(2,1)S(1)} %reshape.149, bf16[]{:T(256)} %constant.15.clone.1), kind=kCustom, calls=%fused_computation.57 | custom fusion | bytes 1026 | tf_op jit(solution)/shard_map/scatter | solution.py:32
  13.3 0.7 all_to_all.20
  14.0 7.6 %all-to-all-start = ((bf16[16,1,32]{2,1,0:T(2,128)(2,1)}), bf16[16,1,32]{2,1,0:T(2,128)(2,1)S(1)}, u32[]{:S(2)}, u32[]{:S(2)}) async-start(bf16[16,1,32]{2,1,0:T(2,128)(2,1)} %all_to_all.20), calls=%async_computation | async-start | bytes 16384 | tf_op jit(solution)/shard_map/all_to_all | solution.py:41
  21.6 1.4 scatter_custom_fusion.1
  23.0 0.1 broadcast_in_dim.28
  23.1 0.0 copy-done
  23.1 4.2 %gather_fusion = bf16[512,3584]{1,0:T(8,128)(2,1)} fusion(bf16[128,3584]{1,0:T(8,128)(2,1)S(1)} %copy-done, s32[1024]{0:T(1024)S(1)} %pad_clamp_fusion.1), kind=kCustom, calls=%fused_computation | custom fusion | bytes 7342080 | tf_op jit(solution)/shard_map/gather | solution.py:30
  27.3 4.1 %broadcast_select_fusion = bf16[16,32,3584]{2,1,0:T(8,128)(2,1)} fusion(bf16[16,32,3584]{2,1,0:T(8,128)(2,1)} %bitcast.42, pred[16,32]{1,0:T(8,128)(4,1)S(1)} %broadcast_in_dim.28), kind=kLoop, calls=%fused_computation.11 | loop fusion | flops 1835008 | bytes 7340544 | tf_op jit(solution)/shard_map/jit(_where)/select_n | solution.py:31
  31.5 0.0 all-to-all-done
  31.5 6.8 %all-to-all-start.1 = ((bf16[16,32,3584]{2,1,0:T(8,128)(2,1)}), bf16[16,32,3584]{2,1,0:T(8,128)(2,1)}, u32[]{:S(2)}, u32[]{:S(2)}) async-start(bf16[16,32,3584]{2,1,0:T(8,128)(2,1)} %broadcast_select_fusion), calls=%async_computation.1 | async-start | bytes 7340032 | tf_op jit(solution)/shard_map/all_to_all | solution.py:34
  38.3 0.0 reduce-scatter.2.cloned.1.call-start
  38.4 0.0 copy-done.2
  38.4 28.6 %pmax.14 = f32[1,1,16]{2,1,0:T(1,128)S(1)} all-reduce(f32[1,1,16]{2,1,0:T(1,128)S(1)} %copy-done.2), channel_id=1, replica_groups=mesh['ed'=16,'ep'=16] {'ed'}, use_global_device_ids=true, to_apply=%region_5.6 | all-reduce | flops 16 | bytes 128 | tf_op jit(solution)/shard_map/pmax | solution.py:56
  67.0 0.6 reduce_max.22
  68.4 0.1 reshape.128
  68.4 22.9 %all-to-all-done.1 = bf16[16,32,3584]{2,1,0:T(8,128)(2,1)} async-done(((bf16[16,32,3584]{2,1,0:T(8,128)(2,1)}), bf16[16,32,3584]{2,1,0:T(8,128)(2,1)}, u32[]{:S(2)}, u32[]{:S(2)}) %all-to-all-start.1) | async-done | bytes 3670048 | tf_op jit(solution)/shard_map/all_to_all | solution.py:34
  91.3 0.0 copy-done.1
  91.3 8.5 %multiply_convert_fusion = bf16[3584,1024]{1,0:T(8,128)(2,1)} fusion(bf16[512,3584]{1,0:T(8,128)(2,1)} %bitcast.4, f32[]{:T(128)} %bitcast.10, f32[512]{0:T(512)S(1)} %reshape.128, bf16[512,2048]{1,0:T(8,128)(2,1)S(1)} %bitcast.50), kind=kOutput, calls=%fused_computation.4 | convolution fusion | flops 3771203584 | bytes 13109252 | tf_op jit(solution)/shard_map/rd,rh->dh/dot_general | solution.py:80
  99.8 0.0 reduce-scatter.2.cloned.1.call-update
  99.8 0.1 slice.19
  99.9 9.7 %fusion.4 = (bf16[512,1024]{1,0:T(8,128)(2,1)S(1)}, bf16[512,1024]{1,0:T(8,128)(2,1)S(1)}, f32[512]{0:T(512)S(1)}) fusion(f32[512]{0:T(512)S(1)} %reshape.128, bf16[512,2048]{1,0:T(8,128)(2,1)} %bitcast.49, bf16[512,3584]{1,0:T(8,128)(2,1)} %bitcast.4, bf16[1,1024,3584]{2,1,0:T(8,128)(2,1)} %param.10), kind=kOutput, calls=%fused_computation.18 | convolution fusion | flops 3769630208 | bytes 15208448 | tf_op jit(solution)/shard_map/rd,hd->rh/dot_general | solution.py:66
  109.6 0.7 all_to_all.18
  110.3 3.9 %all-to-all-start.2 = ((f32[16,1,32]{2,1,0:T(1,128)}), f32[16,1,32]{2,1,0:T(1,128)S(1)}, u32[]{:S(2)}, u32[]{:S(2)}) async-start(f32[16,1,32]{2,1,0:T(1,128)} %all_to_all.18), calls=%async_computation.3 | async-start | bytes 16384 | tf_op jit(solution)/shard_map/all_to_all | solution.py:95
  114.3 1.5 pad_maximum_fusion
  115.8 4.8 %all-to-all-done.2 = f32[16,1,32]{2,1,0:T(1,128)S(1)} async-done(((f32[16,1,32]{2,1,0:T(1,128)}), f32[16,1,32]{2,1,0:T(1,128)S(1)}, u32[]{:S(2)}, u32[]{:S(2)}) %all-to-all-start.2) | async-done | bytes 2080 | tf_op jit(solution)/shard_map/all_to_all | solution.py:95
  120.6 0.5 broadcast.110
  121.1 0.7 reduce.13
  121.8 0.1 reshape.126
  121.9 1.9 gather_fusion.1
  123.8 0.1 reshape.127
  124.0 0.6 copy.22
  124.6 43.0 %reduce-scatter.2.cloned.1.call-done = bf16[224,1024]{1,0:T(8,128)(2,1)} async-done(((bf16[3584,1024]{1,0:T(8,128)(2,1)}), bf16[224,1024]{1,0:T(8,128)(2,1)}) %reduce-scatter.2.cloned.1.call-update) | async-done | bytes 458768 | tf_op jit(solution)/shard_map/reduce_scatter | solution.py:82
  167.6 1.7 fusion.16
  169.3 27.2 %pmax.15 = f32[1]{0:T(128)} all-reduce(f32[1]{0:T(128)} %bitcast.13), channel_id=1, replica_groups=mesh['ed'=16,'ep'=16] {'ed'}, use_global_device_ids=true, to_apply=%region_9.10 | all-reduce | flops 1 | bytes 8 | tf_op jit(solution)/shard_map/pmax | solution.py:90
  197.8 0.6 pad_maximum_fusion.1
  198.4 2.0 convert_bitcast_fusion
  (12 shorter events, 0.1 us)
Async XLA Ops:
  7.2 16.0 %copy-start = (bf16[128,3584]{1,0:T(8,128)(2,1)S(1)}, bf16[128,3584]{1,0:T(8,128)(2,1)}, u32[]{:S(2)}) copy-start(bf16[128,3584]{1,0:T(8,128)(2,1)} %param.6) | copy-start | bytes 2752516
  14.0 17.5 %all-to-all-start = ((bf16[16,1,32]{2,1,0:T(2,128)(2,1)}), bf16[16,1,32]{2,1,0:T(2,128)(2,1)S(1)}, u32[]{:S(2)}, u32[]{:S(2)}) async-start(bf16[16,1,32]{2,1,0:T(2,128)(2,1)} %all_to_all.20), calls=%async_computation | async-start | bytes 16384 | tf_op jit(solution)/shard_map/all_to_all | solution.py:41
  31.5 6.9 %copy-start.2 = (f32[1,1,16]{2,1,0:T(1,128)S(1)}, f32[1,1,16]{2,1,0:T(1,128)}, u32[]{:S(2)}) copy-start(f32[1,1,16]{2,1,0:T(1,128)} %param.11) | copy-start | bytes 196
  31.5 59.8 %copy-start.1 = (bf16[1,1,16,32,2048]{4,3,2,1,0:T(8,128)(2,1)S(1)}, bf16[1,1,16,32,2048]{4,3,2,1,0:T(8,128)(2,1)}, u32[]{:S(2)}) copy-start(bf16[1,1,16,32,2048]{4,3,2,1,0:T(8,128)(2,1)} %param.9) | copy-start | bytes 6291460
  31.5 59.8 %all-to-all-start.1 = ((bf16[16,32,3584]{2,1,0:T(8,128)(2,1)}), bf16[16,32,3584]{2,1,0:T(8,128)(2,1)}, u32[]{:S(2)}, u32[]{:S(2)}) async-start(bf16[16,32,3584]{2,1,0:T(8,128)(2,1)} %broadcast_select_fusion), calls=%async_computation.1 | async-start | bytes 7340032 | tf_op jit(solution)/shard_map/all_to_all | solution.py:34
  38.3 129.3 %reduce-scatter.2.cloned.1.call-start = ((), (), s32[]{:S(2)}) async-start(), calls=%async_computation.4 | async-start | bytes 7798784 | tf_op jit(solution)/shard_map/reduce_scatter | solution.py:82
  110.3 10.3 %all-to-all-start.2 = ((f32[16,1,32]{2,1,0:T(1,128)}), f32[16,1,32]{2,1,0:T(1,128)S(1)}, u32[]{:S(2)}, u32[]{:S(2)}) async-start(f32[16,1,32]{2,1,0:T(1,128)} %all_to_all.18), calls=%async_computation.3 | async-start | bytes 16384 | tf_op jit(solution)/shard_map/all_to_all | solution.py:95
Sparse Core Ops, SparseCore 0:
  100.0 67.6 reduce-scatter.1
where the time goes:
time: 208 us; the launch traced here: 207 us
  waiting for transfers between devices  70.7 us (34%)
  blocking collectives  55.8 us (27%)
  starting transfers between devices  18.4 us (9%)
  matrix products  18.2 us (9%)
  between operations  16.2 us (8%)
  local copies, waits for them, and re-layouts  15.1 us (7%)
  other arithmetic  12.8 us (6%)
    reduce_scatter x1, waiting for transfers between devices, body(): lax.psum_scatter(term(jnp.int32(0), width // n_replicas * lax.axis_size('...  43 us
    pmax x1, blocking collectives, body(): merged = lax.pmax(history, 'ed')[0]  28.6 us
    pmax x1, blocking collectives, body(): peak = lax.pmax(jnp.max(jnp.abs(wgrad), axis=(1, 2)), 'ed')  27.2 us
    all_to_all x1, waiting for transfers between devices, body(): lax.all_to_all(send_rows.reshape(n_ep, local * cap, width), 'ep', split_a...  22.9 us
    dot_general x1, matrix products, body(): jnp.einsum('rd,hd->rh', rows, weight, preferred_element_type=jnp.float32)  9.69 us
    dot_general x1, matrix products, term(): jnp.einsum('rd,rh->dh', rows, weighted, preferred_element_type=jnp.float32)  8.51 us
    all_to_all x1, starting transfers between devices, body(): lax.all_to_all(send_gate.reshape(n_ep, local * cap), 'ep', split_axis=0,...  7.58 us
    all_to_all x1, starting transfers between devices, body(): lax.all_to_all(send_rows.reshape(n_ep, local * cap, width), 'ep', split_a...  6.84 us
  transfers between devices with their start and end apart: 4, of which 3 were waited for; matrix products, arithmetic and copies ran while one was open for 12% of the time, Pallas kernels for 0%

commit v1 on v0

v1 whole, which is shorter than its diff:
```python
import functools

import jax
import jax.numpy as jnp
from jax import lax
from jax.experimental import pallas as pl
from jax.experimental.pallas import tpu as pltpu
from jax.sharding import PartitionSpec as P

LANES = 128
BF16 = jnp.bfloat16
F32 = jnp.float32
HOPS = (4, 3, -3, 2, -2, 1, -1, 0)


def block_order(size):
    me = lax.axis_index("ed")
    place, core = me // 2, me % 2
    spots = [2 * lax.rem(place + hop + size, size // 2) for hop in HOPS]
    return [spot + 1 - core for spot in spots] + [spot + core for spot in spots]


def dispatch_kernel(cap, routes_any, gates_any, grad_any, send_ref, hot0_ref, hot1_ref, routes_ref, gates_ref, grad_ref, held, sems):
    copies = [
        pltpu.make_async_copy(src, dst, sems.at[i])
        for i, (src, dst) in enumerate(
            [(routes_any, routes_ref), (gates_any, gates_ref), (grad_any, grad_ref)]
        )
    ]
    for copy in copies:
        copy.start()
    tokens, width = grad_ref.shape
    blocks = held.shape[0]
    block = width // blocks
    experts = send_ref.shape[0] // cap
    copies[0].wait()
    copies[1].wait()
    expert = lax.broadcasted_iota(jnp.int32, (experts, tokens), 0)
    one = routes_ref[0:1, :] == expert
    two = routes_ref[1:2, :] == expert
    named = jnp.where(one | two, 1.0, 0.0).astype(BF16)
    earlier = lax.broadcasted_iota(jnp.int32, (tokens, tokens), 0) < lax.broadcasted_iota(
        jnp.int32, (tokens, tokens), 1
    )
    before = jnp.dot(named, jnp.where(earlier, 1.0, 0.0).astype(BF16), preferred_element_type=F32)
    slots = lax.broadcasted_iota(jnp.int32, (experts, cap, tokens), 1)
    hit = slots == before.astype(jnp.int32)[:, None, :]
    gate0 = jnp.where(one, gates_ref[0:1, :].astype(F32), 0.0)
    gate1 = jnp.where(two, gates_ref[1:2, :].astype(F32), 0.0)
    rows = experts * cap
    hot0 = jnp.where(hit, jnp.where(one, 1.0, 0.0)[:, None, :], 0.0).reshape(rows, tokens)
    hot1 = jnp.where(hit, jnp.where(two, 1.0, 0.0)[:, None, :], 0.0).reshape(rows, tokens)
    gate = jnp.where(hit, (gate0 + gate1)[:, None, :], 0.0).reshape(rows, tokens)
    hot0_ref[...] = hot0.astype(BF16)
    hot1_ref[...] = hot1.astype(BF16)
    hot = (hot0 + hot1).astype(BF16)
    send_ref[:, width:] = jnp.dot(
        gate.astype(BF16), jnp.ones((tokens, LANES), BF16), preferred_element_type=F32
    ).astype(BF16)
    copies[2].wait()
    x = grad_ref[...].astype(F32)
    for b in range(blocks):
        held[b, :, :block] = x[:, b * block : (b + 1) * block]
    order = block_order(blocks)
    x = jnp.concatenate([held[i][:, :block] for i in order], axis=1).astype(BF16)
    send_ref[:, :width] = jnp.dot(hot, x, preferred_element_type=F32).astype(BF16)


def raw_kernel(rows_ref, pre_ref, weight_ref, grad_ref, score_ref, held):
    hidden, width = weight_ref.shape
    blocks = held.shape[0]
    block = width // blocks
    x = rows_ref[...].astype(F32)
    for i, b in enumerate(block_order(blocks)):
        held[b, :, :block] = x[:, i * block : (i + 1) * block]
    rows = jnp.concatenate([held[b][:, :block] for b in range(blocks)], axis=1).astype(BF16)
    gate = x[:, width : width + 1]
    score = None
    step = 256
    for n in range(0, hidden, step):
        raw = lax.dot_general(
            rows, weight_ref[n : n + step, :], (((1,), (1,)), ((), ())), preferred_element_type=F32
        )
        gate_pre = pre_ref[:, n : n + step].astype(F32)
        up_pre = pre_ref[:, hidden + n : hidden + n + step].astype(F32)
        sigma = jax.nn.sigmoid(gate_pre)
        swish = gate_pre * sigma
        act = (swish * up_pre).astype(BF16).astype(F32)
        part = jnp.sum(act * raw, axis=1, keepdims=True)
        score = part if score is None else score + part
        grad_act = gate * raw
        grad_gate = grad_act * up_pre * sigma * (1.0 + gate_pre * (1.0 - sigma))
        grad_ref[:, n : n + step] = grad_gate.astype(BF16)
        grad_ref[:, hidden + n : hidden + n + step] = (grad_act * swish).astype(BF16)
    score_ref[...] = jnp.broadcast_to(score, score_ref.shape)


def finish_kernel(history_ref, mine_ref, theirs_ref, right_ref, left_ref, out_ref, note_ref):
    acc = mine_ref[...].astype(F32) + theirs_ref[...].astype(F32)
    acc = (acc + right_ref[...].astype(F32)) + left_ref[...].astype(F32)
    out_ref[...] = acc
    peak = jnp.max(jnp.max(jnp.abs(acc), axis=0, keepdims=True), axis=1, keepdims=True)
    hist = history_ref[...]
    rest = jnp.broadcast_to(peak, (1, note_ref.shape[1] - hist.shape[1]))
    note_ref[...] = jnp.broadcast_to(jnp.concatenate([hist, rest], axis=1), note_ref.shape)


def scale_kernel(notes_ref, sum_ref, out_ref, history_ref):
    count = history_ref.shape[1]
    best = jnp.max(notes_ref[...], axis=0, keepdims=True)
    merged, peak = best[:, :count], best[:, count : count + 1]
    ref_amax = jnp.max(merged, axis=1, keepdims=True)
    scale = 1.0 / ref_amax
    out_ref[...] = sum_ref[...] * scale
    history_ref[...] = jnp.concatenate([merged[:, 1:], peak * scale * ref_amax], axis=1)


def whole(memory=pltpu.VMEM):
    return pl.BlockSpec(memory_space=memory)


def dispatch(routes, gates, grad, experts, cap, blocks):
    tokens, width = grad.shape
    block = pl.cdiv(width // blocks, LANES) * LANES
    rows = experts * cap
    return pl.pallas_call(
        functools.partial(dispatch_kernel, cap),
        out_shape=[
            jax.ShapeDtypeStruct((rows, width + LANES), BF16),
            jax.ShapeDtypeStruct((rows, tokens), BF16),
            jax.ShapeDtypeStruct((rows, tokens), BF16),
        ],
        in_specs=[whole(pl.ANY)] * 3,
        out_specs=[whole()] * 3,
        scratch_shapes=[
            pltpu.VMEM(routes.shape, routes.dtype),
            pltpu.VMEM(gates.shape, gates.dtype),
            pltpu.VMEM(grad.shape, grad.dtype),
            pltpu.VMEM((blocks, tokens, block), F32),
            pltpu.SemaphoreType.DMA((3,)),
        ],
        compiler_params=pltpu.CompilerParams(vmem_limit_bytes=16 << 20),
        name="dispatch",
    )(routes, gates, grad)


def gradients(rows, pre, weight, blocks):
    count = rows.shape[0]
    hidden, width = weight.shape
    tile = 256
    block = pl.cdiv(width // blocks, LANES) * LANES
    return pl.pallas_call(
        raw_kernel,
        grid=(count // tile,),
        out_shape=[
            jax.ShapeDtypeStruct(pre.shape, BF16),
            jax.ShapeDtypeStruct((count, LANES), F32),
        ],
        in_specs=[
            pl.BlockSpec((tile, rows.shape[1]), lambda i: (i, 0)),
            pl.BlockSpec((tile, pre.shape[1]), lambda i: (i, 0)),
            pl.BlockSpec((hidden, width), lambda i: (0, 0), pipeline_mode=pl.Buffered(1)),
        ],
        out_specs=[
            pl.BlockSpec((tile, pre.shape[1]), lambda i: (i, 0)),
            pl.BlockSpec((tile, LANES), lambda i: (i, 0)),
        ],
        scratch_shapes=[pltpu.VMEM((blocks, tile, block), F32)],
        compiler_params=pltpu.CompilerParams(vmem_limit_bytes=32 << 20),
        cost_estimate=pl.CostEstimate(
            flops=2 * count * hidden * width, bytes_accessed=12 << 20, transcendentals=0
        ),
        name="gradients",
    )(rows, pre, weight)


def finish(history, mine, theirs, right, left, n_ed):
    return pl.pallas_call(
        finish_kernel,
        out_shape=[
            jax.ShapeDtypeStruct(mine.shape, F32),
            jax.ShapeDtypeStruct((n_ed, LANES), F32),
        ],
        in_specs=[whole()] * 5,
        out_specs=[whole(), whole()],
        compiler_params=pltpu.CompilerParams(vmem_limit_bytes=16 << 20),
        name="finish",
    )(history, mine, theirs, right, left)


def scaled(notes, summed, count):
    return pl.pallas_call(
        scale_kernel,
        out_shape=[
            jax.ShapeDtypeStruct(summed.shape, F32),
            jax.ShapeDtypeStruct((1, count), F32),
        ],
        in_specs=[whole()] * 2,
        out_specs=[whole()] * 2,
        compiler_params=pltpu.CompilerParams(vmem_limit_bytes=16 << 20),
        name="scaled",
    )(notes, summed)


def tie(*values):
    return lax.optimization_barrier(values)


def swap(x, size):
    return lax.ppermute(x, "ed", [(i, i ^ 1) for i in range(size)])


def shift(x, by, size):
    return lax.ppermute(x, "ed", [(i, (i + 2 * by) % size) for i in range(size)])


def both(right, left, size):
    right, left = tie(right, left)
    return shift(right, 1, size), shift(left, -1, size)


def total(*terms):
    acc = terms[0].astype(F32)
    for term in terms[1:]:
        acc = acc + term.astype(F32)
    return acc.astype(BF16)


def body(out_grad, routes, gates, pre_acts, down_weight, history):
    n_src, cap = pre_acts.shape[2], pre_acts.shape[3]
    width_ff, width = down_weight.shape[1:]
    n_ep = lax.axis_size("ep")
    n_ed = lax.axis_size("ed")
    rows_in = n_src * cap
    rows = width // n_ed

    def exchange(x):
        moved = lax.all_to_all(
            x.reshape(n_ep, cap, x.shape[1]), "ep", split_axis=0, concat_axis=0, tiled=True
        )
        return moved.reshape(rows_in, x.shape[1])

    send, hot0, hot1 = dispatch(routes.T, gates.T, out_grad, n_ep, cap, n_ed)
    arrived = exchange(send)
    arrived, pre_acts, down_weight, history = tie(arrived, pre_acts, down_weight, history)

    pre_block = pre_acts[0, 0].reshape(rows_in, 2 * width_ff)
    gate_pre = pre_block[:, :width_ff].astype(F32)
    act = (gate_pre * jax.nn.sigmoid(gate_pre) * pre_block[:, width_ff:].astype(F32)).astype(BF16)
    gate_row = arrived[:, width : width + 1].astype(F32)
    weighted = lax.optimization_barrier((gate_row * act.astype(F32)).astype(BF16))

    half = n_ed // 4 * rows

    def term(index):
        return (
            jnp.einsum(
                "rd,rh->dh",
                arrived[:, index * half : (index + 1) * half],
                weighted,
                preferred_element_type=F32,
            )
            .astype(BF16)
            .reshape(n_ed // 4, rows, width_ff)
        )

    theirs_a = swap(term(0), n_ed)
    mine_a = term(2)
    cut = rows // 2
    start = total(mine_a[0], theirs_a[0])
    right, left = both(start[:cut], start[cut:], n_ed)
    theirs_b = swap(term(1), n_ed)
    mine_b = term(3)
    right, left, theirs_b, mine_b, arrived = tie(right, left, theirs_b, mine_b, arrived)

    right = jnp.pad(right, ((0, rows - cut), (0, 0)))
    left = jnp.pad(left, ((cut, 0), (0, 0)))
    right, left = both(
        total(mine_a[1], theirs_a[1], right), total(mine_a[2], theirs_a[2], left), n_ed
    )
    pre_grad, score = gradients(arrived, pre_block, down_weight[0], n_ed)
    right, left, score = tie(right, left, score)

    right, left = both(
        total(mine_a[3], theirs_a[3], right), total(mine_b[0], theirs_b[0], left), n_ed
    )
    returned = exchange(score)
    right, left, returned = tie(right, left, returned)
    right, left = both(
        total(mine_b[1], theirs_b[1], right), total(mine_b[2], theirs_b[2], left), n_ed
    )
    gate_grad = jnp.stack(
        [jnp.sum(hot0.astype(F32) * returned, axis=0), jnp.sum(hot1.astype(F32) * returned, axis=0)]
    ).T
    right, left, gate_grad = tie(right, left, gate_grad)

    summed, note = finish(history[0], mine_b[3], theirs_b[3], right, left, n_ed)
    notes = lax.all_to_all(note, "ed", split_axis=0, concat_axis=0, tiled=True)
    wgrad, new_history = scaled(notes, summed, history.shape[2])
    return (pre_grad.reshape(pre_acts.shape), wgrad[None], new_history, gate_grad)


def solution(mesh):
    placed = (
        P(("ed", "ep"), None),
        P(("ed", "ep"), None),
        P(("ed", "ep"), None),
        P("ed", "ep", None, None, None),
        P("ep", None, None),
        P("ed", "ep", None),
    )
    return jax.shard_map(
        body,
        mesh=mesh,
        in_specs=placed,
        out_specs=(
            P("ed", "ep", None, None, None),
            P("ep", "ed", None),
            P("ep", None),
            P(("ed", "ep"), None),
        ),
        check_vma=False,
    )
```

time: 208 us -> 132 us (0.63)
  waiting for transfers between devices: 70.7 us -> 13.9 us
  blocking collectives: 55.8 us -> 79.9 us
  between operations: 16.2 us -> 0.79 us
  matrix products: 18.2 us -> 4.57 us
  local copies, waits for them, and re-layouts: 15.1 us -> 2.62 us
  Pallas kernels: 0 us -> 10.9 us
  other arithmetic: 12.8 us -> 3.09 us
  starting transfers between devices: 18.4 us -> 16.3 us
    all_to_all x0 -> x3, blocking collectives: none -> 79.9 us  [the longest x2 63.4 us: exchange(): lax.all_to_all(x.reshape(n_ep, cap, x.shape[1]), 'ep', split_axis=0, conc...]
    pmax x2 -> x0, blocking collectives: 55.8 us -> none  [the longest x1 28.6 us: body(): merged = lax.pmax(history, 'ed')[0]]
    reduce_scatter x1 -> x0, waiting for transfers between devices: 43 us -> none  [body(): lax.psum_scatter(term(jnp.int32(0), width // n_replicas * lax.axis_size('...]
    all_to_all x3 -> x0, waiting for transfers between devices: 27.7 us -> none  [the longest x1 22.9 us: body(): lax.all_to_all(send_rows.reshape(n_ep, local * cap, width), 'ep', split_a...]
    all_to_all x3 -> x0, starting transfers between devices: 18.4 us -> none  [the longest x1 7.58 us: body(): lax.all_to_all(send_gate.reshape(n_ep, local * cap), 'ep', split_axis=0,...]
    ppermute x0 -> x10, starting transfers between devices: none -> 16.3 us  [the longest x8 14 us: shift(): lax.ppermute(x, 'ed', [(i, (i + 2 * by) % size) for i in range(size)])]
    ppermute x0 -> x10, waiting for transfers between devices: none -> 13.9 us  [the longest x8 12.8 us: shift(): lax.ppermute(x, 'ed', [(i, (i + 2 * by) % size) for i in range(size)])]
    dot_general x2 -> x4, matrix products: 18.2 us -> 4.57 us  [term(): jnp.einsum('rd,rh->dh', arrived[:, index * half:(index + 1) * half], weig...]
  transfers between devices with their start and end apart: 4 -> 10, of which waited for: 3 -> 4; matrix products, arithmetic and copies ran while one was open for 12% -> 3% of each run, Pallas kernels for 0% -> 6%
where the time goes in v1:
time: 132 us
  blocking collectives  79.9 us (61%)
  starting transfers between devices  16.3 us (12%)
  waiting for transfers between devices  13.9 us (11%)
  Pallas kernels  10.9 us (8%)
  matrix products  4.57 us (3%)
  other arithmetic  3.09 us (2%)
  local copies, waits for them, and re-layouts  2.62 us (2%)
    all_to_all x2, blocking collectives, exchange(): lax.all_to_all(x.reshape(n_ep, cap, x.shape[1]), 'ep', split_axis=0, conc...  63.4 us
    all_to_all x1, blocking collectives, body(): notes = lax.all_to_all(note, 'ed', split_axis=0, concat_axis=0, tiled=True)  16.5 us
    ppermute x8, starting transfers between devices, shift(): lax.ppermute(x, 'ed', [(i, (i + 2 * by) % size) for i in range(size)])  14 us
    ppermute x8, waiting for transfers between devices, shift(): lax.ppermute(x, 'ed', [(i, (i + 2 * by) % size) for i in range(size)])  12.8 us
    pallas_call x1, Pallas kernels, gradients(): pl.pallas_call(raw_kernel, grid=(count // tile,), out_shape=[jax.ShapeDty...  7.38 us
    dot_general x4, matrix products, term(): jnp.einsum('rd,rh->dh', arrived[:, index * half:(index + 1) * half], weig...  4.57 us
  transfers between devices with their start and end apart: 10, of which 4 were waited for; matrix products, arithmetic and copies ran while one was open for 3% of the time, Pallas kernels for 6%

profile of v1, /device:TPU:1, one launch (start us, length us, event | category | flops | bytes accessed | tf_op | source)
XLA Modules:
  0.0 132.1 jit_solution(5100429278461552843)
XLA Ops:
  0.6 0.0 copy-start.1
  0.6 1.2 copy-done.1
  1.8 0.7 copy-done.2
  2.5 0.7 copy-done.3
  3.1 2.1 %dispatch.1 = (bf16[512,3712]{1,0:T(8,128)(2,1)S(1)}, bf16[512,128]{1,0:T(8,128)(2,1)S(1)}, bf16[512,128]{1,0:T(8,128)(2,1)S(1)}) custom-call(s32[2,128]{1,0:T(2,128)S(1)} %bitcast.74, bf16[2,128]{1,0:T(2,128)(2,1)S(1)} %bitcast.75, bf16[128,3584]{1,0:T(8,128)(2,1)S(1)} %copy-done.1), custom_call_target="tpu_custom_call" | custom-call | tf_op jit(solution)/shard_map/dispatch/pallas_call | solution.py:126
  5.3 0.0 copy-start
  5.3 53.0 %all_to_all.21 = bf16[16,32,3712]{2,1,0:T(8,128)(2,1)S(1)} all-to-all(bf16[16,32,3712]{2,1,0:T(8,128)(2,1)S(1)} %bitcast.68), channel_id=1, replica_groups=mesh['ed'=16,'ep'=16] {'ep'}, dimensions={0} | all-to-all | bytes 7602176 | tf_op jit(solution)/shard_map/all_to_all | solution.py:238
  58.3 0.1 convert_reduce_fusion
  58.4 0.0 copy-done
  58.4 0.7 multiply_convert_fusion
  59.1 1.1 convolution_convert_fusion.2
  60.3 2.2 %collective-permute-start = (bf16[4,224,1024]{2,1,0:T(8,128)(2,1)S(1)}, bf16[4,224,1024]{2,1,0:T(8,128)(2,1)S(1)}, u32[]{:S(2)}, u32[]{:S(2)}) collective-permute-start(bf16[4,224,1024]{2,1,0:T(8,128)(2,1)S(1)} %bitcast.87), channel_id=1, source_target_pairs={{0,16},{16,0},{32,48},{48,32},{64,80},{80,64},{96,112},{112,96},{1... | collective-permute-start | bytes 5505032 | tf_op jit(solution)/shard_map/ppermute | solution.py:210
  62.4 1.1 convolution_convert_fusion.1
  63.6 0.1 collective-permute-start.3
  63.7 1.1 convolution_convert_fusion.3
  64.8 1.0 collective-permute-done
  65.9 0.2 fusion.11
  66.1 0.0 slice-start.1
  66.1 1.7 %collective-permute-start.1 = (bf16[112,1024]{1,0:T(8,128)(2,1)S(1)}, bf16[112,1024]{1,0:T(8,128)(2,1)S(1)}, u32[]{:S(2)}, u32[]{:S(2)}) collective-permute-start(bf16[112,1024]{1,0:T(8,128)(2,1)S(1)} %get-tuple-element.42), channel_id=1, source_target_pairs={{0,32},{16,48},{32,64},{48,80},{64,96},{80,112},{96,128},{112,144}... | collective-permute-start | bytes 688136 | tf_op jit(solution)/shard_map/ppermute | solution.py:214
  67.8 4.0 %collective-permute-start.2 = (bf16[112,1024]{1,0:T(8,128)(2,1)S(1)}, bf16[112,1024]{1,0:T(8,128)(2,1)S(1)}, u32[]{:S(2)}, u32[]{:S(2)}) collective-permute-start(bf16[112,1024]{1,0:T(8,128)(2,1)S(1)} %get-tuple-element.43), channel_id=1, source_target_pairs={{0,224},{16,240},{32,0},{48,16},{64,32},{80,48},{96,64},{112,80},{... | collective-permute-start | bytes 688136 | tf_op jit(solution)/shard_map/ppermute | solution.py:214
  71.8 1.1 convolution_convert_fusion
  73.0 0.0 collective-permute-done.3
  73.0 4.4 %collective-permute-done.1 = bf16[112,1024]{1,0:T(8,128)(2,1)S(1)} collective-permute-done((bf16[112,1024]{1,0:T(8,128)(2,1)S(1)}, bf16[112,1024]{1,0:T(8,128)(2,1)S(1)}, u32[]{:S(2)}, u32[]{:S(2)}) %collective-permute-start.1) | collective-permute-done | bytes 229408 | tf_op jit(solution)/shard_map/ppermute | solution.py:214
  77.4 0.0 collective-permute-done.2
  77.4 0.4 fusion.6
  77.9 0.1 collective-permute-start.4
  77.9 2.7 %collective-permute-start.5 = (bf16[224,1024]{1,0:T(8,128)(2,1)S(1)}, bf16[224,1024]{1,0:T(8,128)(2,1)S(1)}, u32[]{:S(2)}, u32[]{:S(2)}) collective-permute-start(bf16[224,1024]{1,0:T(8,128)(2,1)S(1)} %get-tuple-element.53), channel_id=1, source_target_pairs={{0,224},{16,240},{32,0},{48,16},{64,32},{80,48},{96,64},{112,80},{... | collective-permute-start | bytes 1376264 | tf_op jit(solution)/shard_map/ppermute | solution.py:214
  80.6 7.4 %gradients.1 = (bf16[512,2048]{1,0:T(8,128)(2,1)}, f32[512,128]{1,0:T(8,128)S(1)}) custom-call(bf16[512,3712]{1,0:T(8,128)(2,1)S(1)} %bitcast.67, bf16[512,2048]{1,0:T(8,128)(2,1)S(1)} %bitcast.70, bf16[1024,3584]{1,0:T(8,128)(2,1)S(1)} %bitcast.79), custom_call_target="tpu_custom_call" | custom-call | flops 3758096384 | bytes 12582912 | tf_op jit(solution)/shard_map/gradients/pallas_call | solution.py:152
  88.0 2.3 %collective-permute-done.4 = bf16[224,1024]{1,0:T(8,128)(2,1)S(1)} collective-permute-done((bf16[224,1024]{1,0:T(8,128)(2,1)S(1)}, bf16[224,1024]{1,0:T(8,128)(2,1)S(1)}, u32[]{:S(2)}, u32[]{:S(2)}) %collective-permute-start.4) | collective-permute-done | bytes 458784 | tf_op jit(solution)/shard_map/ppermute | solution.py:214
  90.3 0.0 collective-permute-done.5
  90.3 0.5 fusion.10
  90.8 0.9 collective-permute-start.6
  91.8 1.8 %collective-permute-start.7 = (bf16[224,1024]{1,0:T(8,128)(2,1)S(1)}, bf16[224,1024]{1,0:T(8,128)(2,1)S(1)}, u32[]{:S(2)}, u32[]{:S(2)}) collective-permute-start(bf16[224,1024]{1,0:T(8,128)(2,1)S(1)} %get-tuple-element.58), channel_id=1, source_target_pairs={{0,224},{16,240},{32,0},{48,16},{64,32},{80,48},{96,64},{112,80},{... | collective-permute-start | bytes 1376264 | tf_op jit(solution)/shard_map/ppermute | solution.py:214
  93.6 10.4 %all_to_all.22 = f32[16,32,128]{2,1,0:T(8,128)S(1)} all-to-all(f32[16,32,128]{2,1,0:T(8,128)S(1)} %bitcast.71), channel_id=1, replica_groups=mesh['ed'=16,'ep'=16] {'ep'}, dimensions={0} | all-to-all | bytes 524288 | tf_op jit(solution)/shard_map/all_to_all | solution.py:238
  104.0 0.0 collective-permute-done.6
  104.0 0.0 collective-permute-done.7
  104.0 0.5 fusion.12
  104.5 0.0 copy-start.4
  104.6 0.1 collective-permute-start.8
  104.6 2.7 %collective-permute-start.9 = (bf16[224,1024]{1,0:T(8,128)(2,1)S(1)}, bf16[224,1024]{1,0:T(8,128)(2,1)S(1)}, u32[]{:S(2)}, u32[]{:S(2)}) collective-permute-start(bf16[224,1024]{1,0:T(8,128)(2,1)S(1)} %get-tuple-element.63), channel_id=1, source_target_pairs={{0,224},{16,240},{32,0},{48,16},{64,32},{80,48},{96,64},{112,80},{... | collective-permute-start | bytes 1376264 | tf_op jit(solution)/shard_map/ppermute | solution.py:214
  107.3 0.1 slice_bitcast_fusion.4
  107.4 0.1 multiply_reduce_fusion.1
  107.5 0.6 maximum_bitcast_fusion
  108.0 6.1 %collective-permute-done.8.right_ref = bf16[224,1024]{1,0:T(8,128)(2,1)S(1)} collective-permute-done((bf16[224,1024]{1,0:T(8,128)(2,1)S(1)}, bf16[224,1024]{1,0:T(8,128)(2,1)S(1)}, u32[]{:S(2)}, u32[]{:S(2)}) %collective-permute-start.8) | collective-permute-done | bytes 458784 | tf_op jit(solution)/shard_map/ppermute | solution.py:214
  114.2 0.0 collective-permute-done.9.left_ref
  114.2 0.3 finish.1
  114.5 16.5 %all_to_all.23 = f32[16,1,128]{2,1,0:T(1,128)S(1)} all-to-all(f32[16,1,128]{2,1,0:T(1,128)S(1)} %bitcast.73), channel_id=1, replica_groups=mesh['ed'=16,'ep'=16] {'ed'}, dimensions={0} | all-to-all | bytes 16384 | tf_op jit(solution)/shard_map/all_to_all | solution.py:298
  131.0 1.1 scaled.1
  (8 shorter events, 0.0 us)
Async XLA Ops:
  0.6 1.2 copy-start.1
  1.8 0.7 copy-start.2
  2.5 0.7 copy-start.3
  5.3 53.1 %copy-start = (bf16[1,1,16,32,2048]{4,3,2,1,0:T(8,128)(2,1)S(1)}, bf16[1,1,16,32,2048]{4,3,2,1,0:T(8,128)(2,1)}, u32[]{:S(2)}) copy-start(bf16[1,1,16,32,2048]{4,3,2,1,0:T(8,128)(2,1)} %param.9) | copy-start | bytes 6291460
  60.3 5.6 %collective-permute-start = (bf16[4,224,1024]{2,1,0:T(8,128)(2,1)S(1)}, bf16[4,224,1024]{2,1,0:T(8,128)(2,1)S(1)}, u32[]{:S(2)}, u32[]{:S(2)}) collective-permute-start(bf16[4,224,1024]{2,1,0:T(8,128)(2,1)S(1)} %bitcast.87), channel_id=1, source_target_pairs={{0,16},{16,0},{32,48},{48,32},{64,80},{80,64},{96,112},{112,96},{1... | collective-permute-start | bytes 5505032 | tf_op jit(solution)/shard_map/ppermute | solution.py:210
  63.6 9.4 %collective-permute-start.3 = (bf16[4,224,1024]{2,1,0:T(8,128)(2,1)S(1)}, bf16[4,224,1024]{2,1,0:T(8,128)(2,1)S(1)}, u32[]{:S(2)}, u32[]{:S(2)}) collective-permute-start(bf16[4,224,1024]{2,1,0:T(8,128)(2,1)S(1)} %bitcast.86), channel_id=1, source_target_pairs={{0,16},{16,0},{32,48},{48,32},{64,80},{80,64},{96,112},{112,96},{1... | collective-permute-start | bytes 5505032 | tf_op jit(solution)/shard_map/ppermute | solution.py:210
  65.9 14.8 %slice-start = ((s8[7340032]{0:T(1024)(128)(4,1)}), s8[4194304]{0:T(1024)(128)(4,1)S(1)}, s32[]{:S(2)}) async-start(s8[7340032]{0:T(1024)(128)(4,1)} %bitcast.77), calls=%async_computation.3 | async-start | bytes 8388608
  66.1 14.6 %slice-start.1 = ((s8[7340032]{0:T(1024)(128)(4,1)}), s8[3145728]{0:T(1024)(128)(4,1)S(1)}, s32[]{:S(2)}) async-start(s8[7340032]{0:T(1024)(128)(4,1)} %bitcast.77), calls=%async_computation.4 | async-start | bytes 6291456
  66.1 11.3 %collective-permute-start.1 = (bf16[112,1024]{1,0:T(8,128)(2,1)S(1)}, bf16[112,1024]{1,0:T(8,128)(2,1)S(1)}, u32[]{:S(2)}, u32[]{:S(2)}) collective-permute-start(bf16[112,1024]{1,0:T(8,128)(2,1)S(1)} %get-tuple-element.42), channel_id=1, source_target_pairs={{0,32},{16,48},{32,64},{48,80},{64,96},{80,112},{96,128},{112,144}... | collective-permute-start | bytes 688136 | tf_op jit(solution)/shard_map/ppermute | solution.py:214
  67.8 9.6 %collective-permute-start.2 = (bf16[112,1024]{1,0:T(8,128)(2,1)S(1)}, bf16[112,1024]{1,0:T(8,128)(2,1)S(1)}, u32[]{:S(2)}, u32[]{:S(2)}) collective-permute-start(bf16[112,1024]{1,0:T(8,128)(2,1)S(1)} %get-tuple-element.43), channel_id=1, source_target_pairs={{0,224},{16,240},{32,0},{48,16},{64,32},{80,48},{96,64},{112,80},{... | collective-permute-start | bytes 688136 | tf_op jit(solution)/shard_map/ppermute | solution.py:214
  77.9 12.4 %collective-permute-start.4 = (bf16[224,1024]{1,0:T(8,128)(2,1)S(1)}, bf16[224,1024]{1,0:T(8,128)(2,1)S(1)}, u32[]{:S(2)}, u32[]{:S(2)}) collective-permute-start(bf16[224,1024]{1,0:T(8,128)(2,1)S(1)} %get-tuple-element.52), channel_id=1, source_target_pairs={{0,32},{16,48},{32,64},{48,80},{64,96},{80,112},{96,128},{112,144}... | collective-permute-start | bytes 1376264 | tf_op jit(solution)/shard_map/ppermute | solution.py:214
  77.9 12.4 %collective-permute-start.5 = (bf16[224,1024]{1,0:T(8,128)(2,1)S(1)}, bf16[224,1024]{1,0:T(8,128)(2,1)S(1)}, u32[]{:S(2)}, u32[]{:S(2)}) collective-permute-start(bf16[224,1024]{1,0:T(8,128)(2,1)S(1)} %get-tuple-element.53), channel_id=1, source_target_pairs={{0,224},{16,240},{32,0},{48,16},{64,32},{80,48},{96,64},{112,80},{... | collective-permute-start | bytes 1376264 | tf_op jit(solution)/shard_map/ppermute | solution.py:214
  90.8 13.2 %collective-permute-start.6 = (bf16[224,1024]{1,0:T(8,128)(2,1)S(1)}, bf16[224,1024]{1,0:T(8,128)(2,1)S(1)}, u32[]{:S(2)}, u32[]{:S(2)}) collective-permute-start(bf16[224,1024]{1,0:T(8,128)(2,1)S(1)} %get-tuple-element.57), channel_id=1, source_target_pairs={{0,32},{16,48},{32,64},{48,80},{64,96},{80,112},{96,128},{112,144}... | collective-permute-start | bytes 1376264 | tf_op jit(solution)/shard_map/ppermute | solution.py:214
  91.8 12.2 %collective-permute-start.7 = (bf16[224,1024]{1,0:T(8,128)(2,1)S(1)}, bf16[224,1024]{1,0:T(8,128)(2,1)S(1)}, u32[]{:S(2)}, u32[]{:S(2)}) collective-permute-start(bf16[224,1024]{1,0:T(8,128)(2,1)S(1)} %get-tuple-element.58), channel_id=1, source_target_pairs={{0,224},{16,240},{32,0},{48,16},{64,32},{80,48},{96,64},{112,80},{... | collective-permute-start | bytes 1376264 | tf_op jit(solution)/shard_map/ppermute | solution.py:214
  104.5 9.6 %copy-start.4 = (f32[1,1,16]{2,1,0:T(1,128)S(1)}, f32[1,1,16]{2,1,0:T(1,128)}, u32[]{:S(2)}) copy-start(f32[1,1,16]{2,1,0:T(1,128)} %param.11) | copy-start | bytes 196
  104.6 9.6 %collective-permute-start.8 = (bf16[224,1024]{1,0:T(8,128)(2,1)S(1)}, bf16[224,1024]{1,0:T(8,128)(2,1)S(1)}, u32[]{:S(2)}, u32[]{:S(2)}) collective-permute-start(bf16[224,1024]{1,0:T(8,128)(2,1)S(1)} %get-tuple-element.62), channel_id=1, source_target_pairs={{0,32},{16,48},{32,64},{48,80},{64,96},{80,112},{96,128},{112,144}... | collective-permute-start | bytes 1376264 | tf_op jit(solution)/shard_map/ppermute | solution.py:214
  104.6 9.5 %collective-permute-start.9 = (bf16[224,1024]{1,0:T(8,128)(2,1)S(1)}, bf16[224,1024]{1,0:T(8,128)(2,1)S(1)}, u32[]{:S(2)}, u32[]{:S(2)}) collective-permute-start(bf16[224,1024]{1,0:T(8,128)(2,1)S(1)} %get-tuple-element.63), channel_id=1, source_target_pairs={{0,224},{16,240},{32,0},{48,16},{64,32},{80,48},{96,64},{112,80},{... | collective-permute-start | bytes 1376264 | tf_op jit(solution)/shard_map/ppermute | solution.py:214

commit v2 on v1

--- a/solution.py
+++ b/solution.py
@@ -10,14 +10,24 @@
 LANES = 128
 BF16 = jnp.bfloat16
 F32 = jnp.float32
-HOPS = (4, 3, -3, 2, -2, 1, -1, 0)
 
 
 def block_order(size):
     me = lax.axis_index("ed")
     place, core = me // 2, me % 2
-    spots = [2 * lax.rem(place + hop + size, size // 2) for hop in HOPS]
-    return [spot + 1 - core for spot in spots] + [spot + core for spot in spots]
+
+    def listed(core):
+        up = 1 - 2 * core
+
+        def at(hops, which):
+            return 2 * lax.rem(place + hops + size, size // 2) + which
+
+        blocks = [at(4, core)]
+        for hops in (3, 2, 1):
+            blocks += [at(hops * up, 1 - core), at(hops * up, core)]
+        return blocks + [at(0, core)]
+
+    return listed(1 - core) + listed(core)
 
 
 def dispatch_kernel(cap, routes_any, gates_any, grad_any, send_ref, hot0_ref, hot1_ref, routes_ref, gates_ref, grad_ref, held, sems):
@@ -66,11 +76,65 @@
     send_ref[:, :width] = jnp.dot(hot, x, preferred_element_type=F32).astype(BF16)
 
 
+def term_tiles(rows_ref, weighted, out_ref, first, block):
+    step = 256
+    flat = out_ref.shape[0] * block
+    for c in range(0, flat, step):
+        size = min(step, flat - c)
+        tile = lax.dot_general(
+            rows_ref[:, first + c : first + c + size],
+            weighted,
+            (((0,), (0,)), ((), ())),
+            preferred_element_type=F32,
+        ).astype(BF16)
+        done = 0
+        while done < size:
+            i, j = divmod(c + done, block)
+            count = min(block - j, size - done)
+            out_ref[i, j : j + count, :] = tile[done : done + count]
+            done += count
+
+
+def first_terms_kernel(rows_ref, pre_ref, weighted_ref, theirs_ref, mine_ref):
+    hidden = weighted_ref.shape[1]
+    block = theirs_ref.shape[1]
+    width = rows_ref.shape[1] - LANES
+    gate = rows_ref[:, width:][:, :1].astype(F32)
+    step = 256
+    for n in range(0, hidden, step):
+        gate_pre = pre_ref[:, n : n + step].astype(F32)
+        act = gate_pre * jax.nn.sigmoid(gate_pre) * pre_ref[:, hidden + n : hidden + n + step].astype(F32)
+        weighted_ref[:, n : n + step] = (gate * act.astype(BF16).astype(F32)).astype(BF16)
+    weighted = weighted_ref[...]
+    term_tiles(rows_ref, weighted, theirs_ref, 0, block)
+    term_tiles(rows_ref, weighted, mine_ref, width // 2, block)
+
+
+def more_terms_kernel(first, last, rows_ref, weighted_ref, theirs_ref, mine_ref):
+    block = theirs_ref.shape[1]
+    middle = (rows_ref.shape[1] - LANES) // 2
+    weighted = weighted_ref[...]
+    term_tiles(rows_ref, weighted, theirs_ref, first * block, block)
+    term_tiles(rows_ref, weighted, mine_ref, middle + first * block, block)
+
+
+def open_kernel(mine_ref, theirs_ref, one_ref, two_ref):
+    for i, out_ref in enumerate((one_ref, two_ref)):
+        out_ref[...] = (mine_ref[i].astype(F32) + theirs_ref[i].astype(F32)).astype(BF16)
+
+
+def add_kernel(index, mine_ref, theirs_ref, moved_ref, out_ref):
+    acc = mine_ref[index].astype(F32) + theirs_ref[index].astype(F32)
+    out_ref[...] = (acc + moved_ref[...].astype(F32)).astype(BF16)
+
+
 def raw_kernel(rows_ref, pre_ref, weight_ref, grad_ref, score_ref, held):
     hidden, width = weight_ref.shape
     blocks = held.shape[0]
     block = width // blocks
-    x = rows_ref[...].astype(F32)
+    tile = grad_ref.shape[0]
+    here = pl.ds(pl.multiple_of(pl.program_id(0) * tile, tile), tile)
+    x = rows_ref[here, :].astype(F32)
     for i, b in enumerate(block_order(blocks)):
         held[b, :, :block] = x[:, i * block : (i + 1) * block]
     rows = jnp.concatenate([held[b][:, :block] for b in range(blocks)], axis=1).astype(BF16)
@@ -81,8 +145,8 @@
         raw = lax.dot_general(
             rows, weight_ref[n : n + step, :], (((1,), (1,)), ((), ())), preferred_element_type=F32
         )
-        gate_pre = pre_ref[:, n : n + step].astype(F32)
-        up_pre = pre_ref[:, hidden + n : hidden + n + step].astype(F32)
+        gate_pre = pre_ref[here, n : n + step].astype(F32)
+        up_pre = pre_ref[here, hidden + n : hidden + n + step].astype(F32)
         sigma = jax.nn.sigmoid(gate_pre)
         swish = gate_pre * sigma
         act = (swish * up_pre).astype(BF16).astype(F32)
@@ -96,7 +160,8 @@
 
 
 def finish_kernel(history_ref, mine_ref, theirs_ref, right_ref, left_ref, out_ref, note_ref):
-    acc = mine_ref[...].astype(F32) + theirs_ref[...].astype(F32)
+    last = mine_ref.shape[0] - 1
+    acc = mine_ref[last].astype(F32) + theirs_ref[last].astype(F32)
     acc = (acc + right_ref[...].astype(F32)) + left_ref[...].astype(F32)
     out_ref[...] = acc
     peak = jnp.max(jnp.max(jnp.abs(acc), axis=0, keepdims=True), axis=1, keepdims=True)
@@ -126,11 +191,11 @@
     return pl.pallas_call(
         functools.partial(dispatch_kernel, cap),
         out_shape=[
-            jax.ShapeDtypeStruct((rows, width + LANES), BF16),
-            jax.ShapeDtypeStruct((rows, tokens), BF16),
-            jax.ShapeDtypeStruct((rows, tokens), BF16),
-        ],
-        in_specs=[whole(pl.ANY)] * 3,
+            pltpu.VMEM((rows, width + LANES), BF16),
+            pltpu.VMEM((rows, tokens), BF16),
+            pltpu.VMEM((rows, tokens), BF16),
+        ],
+        in_specs=[whole(pltpu.HBM)] * 3,
         out_specs=[whole()] * 3,
         scratch_shapes=[
             pltpu.VMEM(routes.shape, routes.dtype),
@@ -157,19 +222,17 @@
             jax.ShapeDtypeStruct((count, LANES), F32),
         ],
         in_specs=[
-            pl.BlockSpec((tile, rows.shape[1]), lambda i: (i, 0)),
-            pl.BlockSpec((tile, pre.shape[1]), lambda i: (i, 0)),
-            pl.BlockSpec((hidden, width), lambda i: (0, 0), pipeline_mode=pl.Buffered(1)),
+            whole(),
+            whole(),
+            whole(),
         ],
         out_specs=[
             pl.BlockSpec((tile, pre.shape[1]), lambda i: (i, 0)),
             pl.BlockSpec((tile, LANES), lambda i: (i, 0)),
         ],
         scratch_shapes=[pltpu.VMEM((blocks, tile, block), F32)],
-        compiler_params=pltpu.CompilerParams(vmem_limit_bytes=32 << 20),
-        cost_estimate=pl.CostEstimate(
-            flops=2 * count * hidden * width, bytes_accessed=12 << 20, transcendentals=0
-        ),
+        compiler_params=pltpu.CompilerParams(vmem_limit_bytes=26 << 20),
+        cost_estimate=SMALL,
         name="gradients",
     )(rows, pre, weight)
 
@@ -178,12 +241,13 @@
     return pl.pallas_call(
         finish_kernel,
         out_shape=[
-            jax.ShapeDtypeStruct(mine.shape, F32),
-            jax.ShapeDtypeStruct((n_ed, LANES), F32),
+            pltpu.VMEM(right.shape, F32),
+            pltpu.VMEM((n_ed, LANES), F32),
         ],
         in_specs=[whole()] * 5,
         out_specs=[whole(), whole()],
         compiler_params=pltpu.CompilerParams(vmem_limit_bytes=16 << 20),
+        cost_estimate=SMALL,
         name="finish",
     )(history, mine, theirs, right, left)
 
@@ -202,6 +266,61 @@
     )(notes, summed)
 
 
+LIMIT = 24 << 20
+SMALL = pl.CostEstimate(flops=1 << 10, bytes_accessed=1 << 10, transcendentals=0)
+
+
+def first_terms(rows, pre, block):
+    hidden = pre.shape[1] // 2
+    return pl.pallas_call(
+        first_terms_kernel,
+        out_shape=[pltpu.VMEM((rows.shape[0], hidden), BF16)]
+        + [pltpu.VMEM((2, block, hidden), BF16)] * 2,
+        in_specs=[whole()] * 2,
+        out_specs=[whole()] * 3,
+        compiler_params=pltpu.CompilerParams(vmem_limit_bytes=LIMIT),
+        cost_estimate=SMALL,
+        name="first_terms",
+    )(rows, pre)
+
+
+def more_terms(rows, weighted, first, last, block):
+    hidden = weighted.shape[1]
+    return pl.pallas_call(
+        functools.partial(more_terms_kernel, first, last),
+        out_shape=[pltpu.VMEM((last - first, block, hidden), BF16)] * 2,
+        in_specs=[whole()] * 2,
+        out_specs=[whole()] * 2,
+        compiler_params=pltpu.CompilerParams(vmem_limit_bytes=LIMIT),
+        cost_estimate=SMALL,
+        name="more_terms",
+    )(rows, weighted)
+
+
+def open_sums(mine, theirs):
+    return pl.pallas_call(
+        open_kernel,
+        out_shape=[pltpu.VMEM(mine.shape[1:], BF16)] * 2,
+        in_specs=[whole()] * 2,
+        out_specs=[whole()] * 2,
+        compiler_params=pltpu.CompilerParams(vmem_limit_bytes=LIMIT),
+        cost_estimate=SMALL,
+        name="open_sums",
+    )(mine, theirs)
+
+
+def add(index, mine, theirs, moved):
+    return pl.pallas_call(
+        functools.partial(add_kernel, index),
+        out_shape=pltpu.VMEM(moved.shape, BF16),
+        in_specs=[whole()] * 3,
+        out_specs=whole(),
+        compiler_params=pltpu.CompilerParams(vmem_limit_bytes=LIMIT),
+        cost_estimate=SMALL,
+        name="add",
+    )(mine, theirs, moved)
+
+
 def tie(*values):
     return lax.optimization_barrier(values)
 
@@ -210,20 +329,10 @@
     return lax.ppermute(x, "ed", [(i, i ^ 1) for i in range(size)])
 
 
-def shift(x, by, size):
-    return lax.ppermute(x, "ed", [(i, (i + 2 * by) % size) for i in range(size)])
-
-
-def both(right, left, size):
-    right, left = tie(right, left)
-    return shift(right, 1, size), shift(left, -1, size)
-
-
-def total(*terms):
-    acc = terms[0].astype(F32)
-    for term in terms[1:]:
-        acc = acc + term.astype(F32)
-    return acc.astype(BF16)
+def hop(x, size, cross=0):
+    return lax.ppermute(
+        x, "ed", [(i, ((i + 2 - 4 * (i % 2)) % size) ^ cross) for i in range(size)]
+    )
 
 
 def body(out_grad, routes, gates, pre_acts, down_weight, history):
@@ -240,61 +349,50 @@
         )
         return moved.reshape(rows_in, x.shape[1])
 
-    send, hot0, hot1 = dispatch(routes.T, gates.T, out_grad, n_ep, cap, n_ed)
+    send, hot0, hot1 = dispatch(
+        *[
+            pltpu.with_memory_space_constraint(x, pltpu.HBM)
+            for x in (routes.T, gates.T, out_grad)
+        ],
+        n_ep,
+        cap,
+        n_ed,
+    )
     arrived = exchange(send)
     arrived, pre_acts, down_weight, history = tie(arrived, pre_acts, down_weight, history)
 
     pre_block = pre_acts[0, 0].reshape(rows_in, 2 * width_ff)
-    gate_pre = pre_block[:, :width_ff].astype(F32)
-    act = (gate_pre * jax.nn.sigmoid(gate_pre) * pre_block[:, width_ff:].astype(F32)).astype(BF16)
-    gate_row = arrived[:, width : width + 1].astype(F32)
-    weighted = lax.optimization_barrier((gate_row * act.astype(F32)).astype(BF16))
-
-    half = n_ed // 4 * rows
-
-    def term(index):
-        return (
-            jnp.einsum(
-                "rd,rh->dh",
-                arrived[:, index * half : (index + 1) * half],
-                weighted,
-                preferred_element_type=F32,
-            )
-            .astype(BF16)
-            .reshape(n_ed // 4, rows, width_ff)
-        )
-
-    theirs_a = swap(term(0), n_ed)
-    mine_a = term(2)
-    cut = rows // 2
-    start = total(mine_a[0], theirs_a[0])
-    right, left = both(start[:cut], start[cut:], n_ed)
-    theirs_b = swap(term(1), n_ed)
-    mine_b = term(3)
-    right, left, theirs_b, mine_b, arrived = tie(right, left, theirs_b, mine_b, arrived)
-
-    right = jnp.pad(right, ((0, rows - cut), (0, 0)))
-    left = jnp.pad(left, ((cut, 0), (0, 0)))
-    right, left = both(
-        total(mine_a[1], theirs_a[1], right), total(mine_a[2], theirs_a[2], left), n_ed
-    )
-    pre_grad, score = gradients(arrived, pre_block, down_weight[0], n_ed)
-    right, left, score = tie(right, left, score)
-
-    right, left = both(
-        total(mine_a[3], theirs_a[3], right), total(mine_b[0], theirs_b[0], left), n_ed
-    )
+    arrived, pre_block, weight = [
+        pltpu.with_memory_space_constraint(x, pltpu.VMEM)
+        for x in (arrived, pre_block, down_weight[0])
+    ]
+    weighted, theirs_e, mine_e = first_terms(arrived, pre_block, rows)
+    theirs_e = swap(theirs_e, n_ed)
+    theirs, mine = more_terms(arrived, weighted, 2, n_ed // 2, rows)
+    theirs_e, theirs, mine = tie(theirs_e, theirs, mine)
+    even, odd = open_sums(mine_e, theirs_e)
+    even, odd, theirs, arrived = tie(even, odd, theirs, arrived)
+    even, odd = hop(even, n_ed), hop(odd, n_ed)
+    theirs = swap(theirs, n_ed)
+    pre_grad, score = gradients(arrived, pre_block, weight, n_ed)
+    even, theirs, mine, score = tie(even, theirs, mine, score)
+
+    even = hop(add(0, mine, theirs, even), n_ed)
+    odd = add(1, mine, theirs, odd)
+    odd, score = tie(odd, score)
+    odd = hop(odd, n_ed)
     returned = exchange(score)
-    right, left, returned = tie(right, left, returned)
-    right, left = both(
-        total(mine_b[1], theirs_b[1], right), total(mine_b[2], theirs_b[2], left), n_ed
-    )
+    even, returned = tie(even, returned)
+
+    even = hop(add(2, mine, theirs, even), n_ed)
+    odd = hop(add(3, mine, theirs, odd), n_ed, 1)
     gate_grad = jnp.stack(
         [jnp.sum(hot0.astype(F32) * returned, axis=0), jnp.sum(hot1.astype(F32) * returned, axis=0)]
     ).T
-    right, left, gate_grad = tie(right, left, gate_grad)
-
-    summed, note = finish(history[0], mine_b[3], theirs_b[3], right, left, n_ed)
+    even, gate_grad = tie(even, gate_grad)
+    even = hop(add(4, mine, theirs, even), n_ed)
+
+    summed, note = finish(history[0], mine, theirs, even, odd, n_ed)
     notes = lax.all_to_all(note, "ed", split_axis=0, concat_axis=0, tiled=True)
     wgrad, new_history = scaled(notes, summed, history.shape[2])
     return (pre_grad.reshape(pre_acts.shape), wgrad[None], new_history, gate_grad)

time: 132 us -> 128 us (0.970)
  Pallas kernels: 10.9 us -> 17.8 us
  matrix products: 4.57 us -> 0 us
  local copies, waits for them, and re-layouts: 2.62 us -> 0.02 us
  other arithmetic: 3.09 us -> 0.66 us
  blocking collectives: 79.9 us -> 78.4 us
    pallas_call x2 -> x10, Pallas kernels: 2.44 us -> 9.37 us  [the longest x1 3.43 us: more_terms(): pl.pallas_call(functools.partial(more_terms_kernel, first, last), out_sha...]
    dot_general x4 -> x0, matrix products: 4.57 us -> none  [term(): jnp.einsum('rd,rh->dh', arrived[:, index * half:(index + 1) * half], weig...]
    unnamed x14 -> x8, local copies, waits for them, and re-layouts: 2.53 us -> 0.02 us
    all_to_all x1, blocking collectives: 16.5 us -> 14.1 us  [body(): notes = lax.all_to_all(note, 'ed', split_axis=0, concat_axis=0, tiled=True)]
    convert_element_type x5 -> x0, other arithmetic: 2.31 us -> none  [the longest x4 1.64 us: total(): return acc.astype(BF16)]
    ppermute x8 -> x7, waiting for transfers between devices: 12.8 us -> 13.6 us  [hop(): lax.ppermute(x, 'ed', [(i, (i + 2 - 4 * (i % 2)) % size ^ cross) for i in...]
    ppermute x8 -> x7, starting transfers between devices: 14 us -> 14.5 us  [hop(): lax.ppermute(x, 'ed', [(i, (i + 2 - 4 * (i % 2)) % size ^ cross) for i in...]
  transfers between devices with their start and end apart: 10 -> 9, of which waited for: 4 -> 4; matrix products, arithmetic and copies ran while one was open for 3% -> 1% of each run, Pallas kernels for 6% -> 9%
where the time goes in v2:
time: 128 us
  blocking collectives  78.4 us (61%)
  Pallas kernels  17.8 us (14%)
  starting transfers between devices  16.8 us (13%)
  waiting for transfers between devices  13.6 us (11%)
    all_to_all x2, blocking collectives, exchange(): lax.all_to_all(x.reshape(n_ep, cap, x.shape[1]), 'ep', split_axis=0, conc...  64.3 us
    ppermute x7, starting transfers between devices, hop(): lax.ppermute(x, 'ed', [(i, (i + 2 - 4 * (i % 2)) % size ^ cross) for i in...  14.5 us
    all_to_all x1, blocking collectives, body(): notes = lax.all_to_all(note, 'ed', split_axis=0, concat_axis=0, tiled=True)  14.1 us
    ppermute x7, waiting for transfers between devices, hop(): lax.ppermute(x, 'ed', [(i, (i + 2 - 4 * (i % 2)) % size ^ cross) for i in...  13.6 us
    pallas_call x1, Pallas kernels, gradients(): pl.pallas_call(raw_kernel, grid=(count // tile,), out_shape=[jax.ShapeDty...  7.38 us
    pallas_call x1, Pallas kernels, more_terms(): pl.pallas_call(functools.partial(more_terms_kernel, first, last), out_sha...  3.43 us
    pallas_call x1, Pallas kernels, dispatch(): pl.pallas_call(functools.partial(dispatch_kernel, cap), out_shape=[pltpu....  2.79 us
  transfers between devices with their start and end apart: 9, of which 4 were waited for; matrix products, arithmetic and copies ran while one was open for 1% of the time, Pallas kernels for 9%

profile of v2, /device:TPU:1, one launch (start us, length us, event | category | flops | bytes accessed | tf_op | source)
XLA Modules:
  0.0 128.0 jit_solution(1011921950813172435)
XLA Ops:
  0.6 2.8 %dispatch.1 = (bf16[512,3712]{1,0:T(8,128)(2,1)S(1)}, bf16[512,128]{1,0:T(8,128)(2,1)S(1)}, bf16[512,128]{1,0:T(8,128)(2,1)S(1)}) custom-call(s32[2,128]{1,0:T(2,128)} %bitcast.35, bf16[2,128]{1,0:T(2,128)(2,1)} %bitcast.36, bf16[128,3584]{1,0:T(8,128)(2,1)} %grad_any.1), custom_call_target="tpu_custom_call" | custom-call | tf_op jit(solution)/shard_map/dispatch/pallas_call | solution.py:191
  3.4 0.0 copy-start
  3.4 0.0 slice-start
  3.5 53.2 %all_to_all.21 = bf16[16,32,3712]{2,1,0:T(8,128)(2,1)S(1)} all-to-all(bf16[16,32,3712]{2,1,0:T(8,128)(2,1)S(1)} %bitcast.27), channel_id=1, replica_groups=mesh['ed'=16,'ep'=16] {'ep'}, dimensions={0} | all-to-all | bytes 7602176 | tf_op jit(solution)/shard_map/all_to_all | solution.py:347
  56.6 0.0 copy-done
  56.6 0.0 slice-start.1
  56.6 1.8 %first_terms.1 = (bf16[512,1024]{1,0:T(8,128)(2,1)S(1)}, bf16[2,224,1024]{2,1,0:T(8,128)(2,1)S(1)}, bf16[2,224,1024]{2,1,0:T(8,128)(2,1)S(1)}) custom-call(bf16[512,3712]{1,0:T(8,128)(2,1)S(1)} %bitcast.19, bf16[512,2048]{1,0:T(8,128)(2,1)S(1)} %bitcast.22), custom_call_target="tpu_custom_call" | custom-call | flops 1024 | bytes 1024 | tf_op jit(solution)/shard_map/first_terms/pallas_call | solution.py:275
  58.4 2.2 %collective-permute-start = (bf16[2,224,1024]{2,1,0:T(8,128)(2,1)S(1)}, bf16[2,224,1024]{2,1,0:T(8,128)(2,1)S(1)}, u32[]{:S(2)}, u32[]{:S(2)}) collective-permute-start(bf16[2,224,1024]{2,1,0:T(8,128)(2,1)S(1)} %get-tuple-element.45), channel_id=1, source_target_pairs={{0,16},{16,0},{32,48},{48,32},{64,80},{80,64},{96,112},{112,96},{1... | collective-permute-start | bytes 2752520 | tf_op jit(solution)/shard_map/ppermute | solution.py:329
  60.6 3.4 %more_terms.1 = (bf16[6,224,1024]{2,1,0:T(8,128)(2,1)S(1)}, bf16[6,224,1024]{2,1,0:T(8,128)(2,1)S(1)}) custom-call(bf16[512,3712]{1,0:T(8,128)(2,1)S(1)} %bitcast.20, bf16[512,1024]{1,0:T(8,128)(2,1)S(1)} %get-tuple-element.46.weighted_ref), custom_call_target="tpu_custom_call" | custom-call | flops 1024 | bytes 1024 | tf_op jit(solution)/shard_map/more_terms/pallas_call | solution.py:289
  64.0 0.0 collective-permute-done.theirs_ref
  64.0 0.2 open_sums.1
  64.3 0.1 collective-permute-start.2
  64.4 5.6 %collective-permute-start.1 = (bf16[224,1024]{1,0:T(8,128)(2,1)S(1)}, bf16[224,1024]{1,0:T(8,128)(2,1)S(1)}, u32[]{:S(2)}, u32[]{:S(2)}) collective-permute-start(bf16[224,1024]{1,0:T(8,128)(2,1)S(1)} %get-tuple-element.57), channel_id=1, source_target_pairs={{0,32},{16,240},{32,64},{48,16},{64,96},{80,48},{96,128},{112,80},... | collective-permute-start | bytes 1376264 | tf_op jit(solution)/shard_map/ppermute | solution.py:333
  70.0 0.7 collective-permute-start.4
  70.7 0.0 slice-done
  70.8 0.0 slice-done.1
  70.8 7.4 %gradients.1 = (bf16[512,2048]{1,0:T(8,128)(2,1)}, f32[512,128]{1,0:T(8,128)S(1)}) custom-call(bf16[512,3712]{1,0:T(8,128)(2,1)S(1)} %bitcast.21, bf16[512,2048]{1,0:T(8,128)(2,1)S(1)} %bitcast.23, bf16[1024,3584]{1,0:T(8,128)(2,1)S(1)} %bitcast.26), custom_call_target="tpu_custom_call" | custom-call | flops 1024 | bytes 1024 | tf_op jit(solution)/shard_map/gradients/pallas_call | solution.py:217
  78.1 0.0 collective-permute-done.1.moved_ref
  78.1 0.0 collective-permute-done.2.theirs_ref
  78.1 0.2 add.5
  78.3 0.8 collective-permute-start.3
  79.1 1.2 collective-permute-done.4.moved_ref
  80.4 0.2 add.6
  80.5 3.2 %collective-permute-start.7 = (bf16[224,1024]{1,0:T(8,128)(2,1)S(1)}, bf16[224,1024]{1,0:T(8,128)(2,1)S(1)}, u32[]{:S(2)}, u32[]{:S(2)}) collective-permute-start(bf16[224,1024]{1,0:T(8,128)(2,1)S(1)} %add.6), channel_id=1, source_target_pairs={{0,32},{16,240},{32,64},{48,16},{64,96},{80,48},{96,128},{112,80},... | collective-permute-start | bytes 1376264 | tf_op jit(solution)/shard_map/ppermute | solution.py:333
  83.7 11.1 %all_to_all.22 = f32[16,32,128]{2,1,0:T(8,128)S(1)} all-to-all(f32[16,32,128]{2,1,0:T(8,128)S(1)} %bitcast.28), channel_id=1, replica_groups=mesh['ed'=16,'ep'=16] {'ep'}, dimensions={0} | all-to-all | bytes 524288 | tf_op jit(solution)/shard_map/all_to_all | solution.py:347
  94.8 0.0 collective-permute-done.3.moved_ref
  94.8 0.2 add.7
  95.0 0.1 collective-permute-start.5
  95.1 0.0 collective-permute-done.7.moved_ref
  95.1 0.2 add.9
  95.3 3.0 %collective-permute-start.8 = (bf16[224,1024]{1,0:T(8,128)(2,1)S(1)}, bf16[224,1024]{1,0:T(8,128)(2,1)S(1)}, u32[]{:S(2)}, u32[]{:S(2)}) collective-permute-start(bf16[224,1024]{1,0:T(8,128)(2,1)S(1)} %add.9), channel_id=1, source_target_pairs={{0,48},{16,224},{32,80},{48,0},{64,112},{80,32},{96,144},{112,64},... | collective-permute-start | bytes 1376264 | tf_op jit(solution)/shard_map/ppermute | solution.py:333
  98.3 0.1 multiply_reduce_fusion.1
  98.4 0.6 maximum_bitcast_fusion
  99.0 0.0 copy-start.1
  99.0 3.7 %collective-permute-done.5.moved_ref = bf16[224,1024]{1,0:T(8,128)(2,1)S(1)} collective-permute-done((bf16[224,1024]{1,0:T(8,128)(2,1)S(1)}, bf16[224,1024]{1,0:T(8,128)(2,1)S(1)}, u32[]{:S(2)}, u32[]{:S(2)}) %collective-permute-start.5) | collective-permute-done | bytes 458784 | tf_op jit(solution)/shard_map/ppermute | solution.py:333
  102.7 0.2 add.8
  102.9 1.0 collective-permute-start.6
  103.9 5.2 %collective-permute-done.8.left_ref = bf16[224,1024]{1,0:T(8,128)(2,1)S(1)} collective-permute-done((bf16[224,1024]{1,0:T(8,128)(2,1)S(1)}, bf16[224,1024]{1,0:T(8,128)(2,1)S(1)}, u32[]{:S(2)}, u32[]{:S(2)}) %collective-permute-start.8) | collective-permute-done | bytes 458784 | tf_op jit(solution)/shard_map/ppermute | solution.py:333
  109.1 3.4 %collective-permute-done.6.right_ref = bf16[224,1024]{1,0:T(8,128)(2,1)S(1)} collective-permute-done((bf16[224,1024]{1,0:T(8,128)(2,1)S(1)}, bf16[224,1024]{1,0:T(8,128)(2,1)S(1)}, u32[]{:S(2)}, u32[]{:S(2)}) %collective-permute-start.6) | collective-permute-done | bytes 458784 | tf_op jit(solution)/shard_map/ppermute | solution.py:333
  112.5 0.0 copy-done.1
  112.5 0.3 finish.1
  112.9 14.1 %all_to_all.23 = f32[16,1,128]{2,1,0:T(1,128)S(1)} all-to-all(f32[16,1,128]{2,1,0:T(1,128)S(1)} %bitcast.30), channel_id=1, replica_groups=mesh['ed'=16,'ep'=16] {'ed'}, dimensions={0} | all-to-all | bytes 16384 | tf_op jit(solution)/shard_map/all_to_all | solution.py:396
  127.0 1.1 scaled.1
  (1 shorter events, 0.0 us)
Async XLA Ops:
  3.4 53.2 %copy-start = (bf16[1,1,16,32,2048]{4,3,2,1,0:T(8,128)(2,1)S(1)}, bf16[1,1,16,32,2048]{4,3,2,1,0:T(8,128)(2,1)}, u32[]{:S(2)}) copy-start(bf16[1,1,16,32,2048]{4,3,2,1,0:T(8,128)(2,1)} %param.9) | copy-start | bytes 6291460
  3.4 67.3 %slice-start = ((s8[7340032]{0:T(1024)(128)(4,1)}), s8[4194304]{0:T(1024)(128)(4,1)S(1)}, s32[]{:S(2)}) async-start(s8[7340032]{0:T(1024)(128)(4,1)} %bitcast.24), calls=%async_computation.3 | async-start | bytes 8388608
  56.6 14.1 %slice-start.1 = ((s8[7340032]{0:T(1024)(128)(4,1)}), s8[3145728]{0:T(1024)(128)(4,1)S(1)}, s32[]{:S(2)}) async-start(s8[7340032]{0:T(1024)(128)(4,1)} %bitcast.24), calls=%async_computation.4 | async-start | bytes 6291456
  58.4 5.6 %collective-permute-start = (bf16[2,224,1024]{2,1,0:T(8,128)(2,1)S(1)}, bf16[2,224,1024]{2,1,0:T(8,128)(2,1)S(1)}, u32[]{:S(2)}, u32[]{:S(2)}) collective-permute-start(bf16[2,224,1024]{2,1,0:T(8,128)(2,1)S(1)} %get-tuple-element.45), channel_id=1, source_target_pairs={{0,16},{16,0},{32,48},{48,32},{64,80},{80,64},{96,112},{112,96},{1... | collective-permute-start | bytes 2752520 | tf_op jit(solution)/shard_map/ppermute | solution.py:329
  64.3 13.9 %collective-permute-start.2 = (bf16[6,224,1024]{2,1,0:T(8,128)(2,1)S(1)}, bf16[6,224,1024]{2,1,0:T(8,128)(2,1)S(1)}, u32[]{:S(2)}, u32[]{:S(2)}) collective-permute-start(bf16[6,224,1024]{2,1,0:T(8,128)(2,1)S(1)} %get-tuple-element.58), channel_id=1, source_target_pairs={{0,16},{16,0},{32,48},{48,32},{64,80},{80,64},{96,112},{112,96},{1... | collective-permute-start | bytes 8257544 | tf_op jit(solution)/shard_map/ppermute | solution.py:329
  64.4 13.8 %collective-permute-start.1 = (bf16[224,1024]{1,0:T(8,128)(2,1)S(1)}, bf16[224,1024]{1,0:T(8,128)(2,1)S(1)}, u32[]{:S(2)}, u32[]{:S(2)}) collective-permute-start(bf16[224,1024]{1,0:T(8,128)(2,1)S(1)} %get-tuple-element.57), channel_id=1, source_target_pairs={{0,32},{16,240},{32,64},{48,16},{64,96},{80,48},{96,128},{112,80},... | collective-permute-start | bytes 1376264 | tf_op jit(solution)/shard_map/ppermute | solution.py:333
  70.0 10.3 %collective-permute-start.4 = (bf16[224,1024]{1,0:T(8,128)(2,1)S(1)}, bf16[224,1024]{1,0:T(8,128)(2,1)S(1)}, u32[]{:S(2)}, u32[]{:S(2)}) collective-permute-start(bf16[224,1024]{1,0:T(8,128)(2,1)S(1)} %get-tuple-element.64), channel_id=1, source_target_pairs={{0,32},{16,240},{32,64},{48,16},{64,96},{80,48},{96,128},{112,80},... | collective-permute-start | bytes 1376264 | tf_op jit(solution)/shard_map/ppermute | solution.py:333
  78.3 16.5 %collective-permute-start.3 = (bf16[224,1024]{1,0:T(8,128)(2,1)S(1)}, bf16[224,1024]{1,0:T(8,128)(2,1)S(1)}, u32[]{:S(2)}, u32[]{:S(2)}) collective-permute-start(bf16[224,1024]{1,0:T(8,128)(2,1)S(1)} %add.5), channel_id=1, source_target_pairs={{0,32},{16,240},{32,64},{48,16},{64,96},{80,48},{96,128},{112,80},... | collective-permute-start | bytes 1376264 | tf_op jit(solution)/shard_map/ppermute | solution.py:333
  80.5 14.6 %collective-permute-start.7 = (bf16[224,1024]{1,0:T(8,128)(2,1)S(1)}, bf16[224,1024]{1,0:T(8,128)(2,1)S(1)}, u32[]{:S(2)}, u32[]{:S(2)}) collective-permute-start(bf16[224,1024]{1,0:T(8,128)(2,1)S(1)} %add.6), channel_id=1, source_target_pairs={{0,32},{16,240},{32,64},{48,16},{64,96},{80,48},{96,128},{112,80},... | collective-permute-start | bytes 1376264 | tf_op jit(solution)/shard_map/ppermute | solution.py:333
  95.0 7.7 %collective-permute-start.5 = (bf16[224,1024]{1,0:T(8,128)(2,1)S(1)}, bf16[224,1024]{1,0:T(8,128)(2,1)S(1)}, u32[]{:S(2)}, u32[]{:S(2)}) collective-permute-start(bf16[224,1024]{1,0:T(8,128)(2,1)S(1)} %add.7), channel_id=1, source_target_pairs={{0,32},{16,240},{32,64},{48,16},{64,96},{80,48},{96,128},{112,80},... | collective-permute-start | bytes 1376264 | tf_op jit(solution)/shard_map/ppermute | solution.py:333
  95.3 13.8 %collective-permute-start.8 = (bf16[224,1024]{1,0:T(8,128)(2,1)S(1)}, bf16[224,1024]{1,0:T(8,128)(2,1)S(1)}, u32[]{:S(2)}, u32[]{:S(2)}) collective-permute-start(bf16[224,1024]{1,0:T(8,128)(2,1)S(1)} %add.9), channel_id=1, source_target_pairs={{0,48},{16,224},{32,80},{48,0},{64,112},{80,32},{96,144},{112,64},... | collective-permute-start | bytes 1376264 | tf_op jit(solution)/shard_map/ppermute | solution.py:333
  99.0 13.6 %copy-start.1 = (f32[1,1,16]{2,1,0:T(1,128)S(1)}, f32[1,1,16]{2,1,0:T(1,128)}, u32[]{:S(2)}) copy-start(f32[1,1,16]{2,1,0:T(1,128)} %param.11) | copy-start | bytes 196
  102.9 9.7 %collective-permute-start.6 = (bf16[224,1024]{1,0:T(8,128)(2,1)S(1)}, bf16[224,1024]{1,0:T(8,128)(2,1)S(1)}, u32[]{:S(2)}, u32[]{:S(2)}) collective-permute-start(bf16[224,1024]{1,0:T(8,128)(2,1)S(1)} %add.8), channel_id=1, source_target_pairs={{0,32},{16,240},{32,64},{48,16},{64,96},{80,48},{96,128},{112,80},... | collective-permute-start | bytes 1376264 | tf_op jit(solution)/shard_map/ppermute | solution.py:333

commit v3 on v2

--- a/solution.py
+++ b/solution.py
@@ -30,7 +30,7 @@
     return listed(1 - core) + listed(core)
 
 
-def dispatch_kernel(cap, routes_any, gates_any, grad_any, send_ref, hot0_ref, hot1_ref, routes_ref, gates_ref, grad_ref, held, sems):
+def dispatch_kernel(cap, routes_any, gates_any, grad_any, send_ref, inverse0_ref, inverse1_ref, routes_ref, gates_ref, grad_ref, held, sems):
     copies = [
         pltpu.make_async_copy(src, dst, sems.at[i])
         for i, (src, dst) in enumerate(
@@ -55,25 +55,27 @@
     before = jnp.dot(named, jnp.where(earlier, 1.0, 0.0).astype(BF16), preferred_element_type=F32)
     slots = lax.broadcasted_iota(jnp.int32, (experts, cap, tokens), 1)
     hit = slots == before.astype(jnp.int32)[:, None, :]
-    gate0 = jnp.where(one, gates_ref[0:1, :].astype(F32), 0.0)
-    gate1 = jnp.where(two, gates_ref[1:2, :].astype(F32), 0.0)
+    gate0 = gates_ref[0:1, :].astype(F32)
+    gate1 = gates_ref[1:2, :].astype(F32)
     rows = experts * cap
-    hot0 = jnp.where(hit, jnp.where(one, 1.0, 0.0)[:, None, :], 0.0).reshape(rows, tokens)
-    hot1 = jnp.where(hit, jnp.where(two, 1.0, 0.0)[:, None, :], 0.0).reshape(rows, tokens)
-    gate = jnp.where(hit, (gate0 + gate1)[:, None, :], 0.0).reshape(rows, tokens)
-    hot0_ref[...] = hot0.astype(BF16)
-    hot1_ref[...] = hot1.astype(BF16)
-    hot = (hot0 + hot1).astype(BF16)
-    send_ref[:, width:] = jnp.dot(
-        gate.astype(BF16), jnp.ones((tokens, LANES), BF16), preferred_element_type=F32
-    ).astype(BF16)
+
+    def place(values):
+        return jnp.where(hit, values[:, None, :], 0.0).reshape(rows, tokens)
+
+    inverse0_ref[...] = place(jnp.where(one, 1.0 / gate0, 0.0))
+    inverse1_ref[...] = place(jnp.where(two, 1.0 / gate1, 0.0))
+    gate = place(jnp.where(one, gate0, 0.0) + jnp.where(two, gate1, 0.0)).astype(BF16)
     copies[2].wait()
-    x = grad_ref[...].astype(F32)
+    x = grad_ref[...]
     for b in range(blocks):
         held[b, :, :block] = x[:, b * block : (b + 1) * block]
     order = block_order(blocks)
-    x = jnp.concatenate([held[i][:, :block] for i in order], axis=1).astype(BF16)
-    send_ref[:, :width] = jnp.dot(hot, x, preferred_element_type=F32).astype(BF16)
+    x = jnp.concatenate([held[i][:, :block] for i in order], axis=1)
+    send_ref[...] = jnp.dot(gate, x, preferred_element_type=F32).astype(BF16)
+
+
+def sigmoid(x):
+    return 0.5 * jnp.tanh(0.5 * x) + 0.5
 
 
 def term_tiles(rows_ref, weighted, out_ref, first, block):
@@ -95,27 +97,32 @@
             done += count
 
 
-def first_terms_kernel(rows_ref, pre_ref, weighted_ref, theirs_ref, mine_ref):
-    hidden = weighted_ref.shape[1]
-    block = theirs_ref.shape[1]
-    width = rows_ref.shape[1] - LANES
-    gate = rows_ref[:, width:][:, :1].astype(F32)
+def first_terms_kernel(rows_ref, pre_ref, act_ref, theirs_ref):
+    hidden = act_ref.shape[1]
     step = 256
     for n in range(0, hidden, step):
         gate_pre = pre_ref[:, n : n + step].astype(F32)
-        act = gate_pre * jax.nn.sigmoid(gate_pre) * pre_ref[:, hidden + n : hidden + n + step].astype(F32)
-        weighted_ref[:, n : n + step] = (gate * act.astype(BF16).astype(F32)).astype(BF16)
-    weighted = weighted_ref[...]
-    term_tiles(rows_ref, weighted, theirs_ref, 0, block)
-    term_tiles(rows_ref, weighted, mine_ref, width // 2, block)
-
-
-def more_terms_kernel(first, last, rows_ref, weighted_ref, theirs_ref, mine_ref):
+        up_pre = pre_ref[:, hidden + n : hidden + n + step].astype(F32)
+        act_ref[:, n : n + step] = (gate_pre * sigmoid(gate_pre) * up_pre).astype(BF16)
+    term_tiles(rows_ref, act_ref[...], theirs_ref, 0, theirs_ref.shape[1])
+
+
+def second_terms_kernel(rows_ref, act_ref, early_ref, theirs_ref, mine_ref):
     block = theirs_ref.shape[1]
-    middle = (rows_ref.shape[1] - LANES) // 2
-    weighted = weighted_ref[...]
-    term_tiles(rows_ref, weighted, theirs_ref, first * block, block)
-    term_tiles(rows_ref, weighted, mine_ref, middle + first * block, block)
+    middle = rows_ref.shape[1] // 2
+    act = act_ref[...]
+    term_tiles(rows_ref, act, early_ref, middle, block)
+    first = early_ref.shape[0] * block
+    term_tiles(rows_ref, act, theirs_ref, first, block)
+    term_tiles(rows_ref, act, mine_ref, middle + first, block)
+
+
+def last_terms_kernel(first, rows_ref, act_ref, theirs_ref, mine_ref):
+    block = theirs_ref.shape[1]
+    middle = rows_ref.shape[1] // 2
+    act = act_ref[...]
+    term_tiles(rows_ref, act, theirs_ref, first * block, block)
+    term_tiles(rows_ref, act, mine_ref, middle + first * block, block)
 
 
 def open_kernel(mine_ref, theirs_ref, one_ref, two_ref):
@@ -134,11 +141,10 @@
     block = width // blocks
     tile = grad_ref.shape[0]
     here = pl.ds(pl.multiple_of(pl.program_id(0) * tile, tile), tile)
-    x = rows_ref[here, :].astype(F32)
+    x = rows_ref[here, :]
     for i, b in enumerate(block_order(blocks)):
         held[b, :, :block] = x[:, i * block : (i + 1) * block]
-    rows = jnp.concatenate([held[b][:, :block] for b in range(blocks)], axis=1).astype(BF16)
-    gate = x[:, width : width + 1]
+    rows = jnp.concatenate([held[b][:, :block] for b in range(blocks)], axis=1)
     score = None
     step = 256
     for n in range(0, hidden, step):
@@ -147,15 +153,14 @@
         )
         gate_pre = pre_ref[here, n : n + step].astype(F32)
         up_pre = pre_ref[here, hidden + n : hidden + n + step].astype(F32)
-        sigma = jax.nn.sigmoid(gate_pre)
+        sigma = sigmoid(gate_pre)
         swish = gate_pre * sigma
         act = (swish * up_pre).astype(BF16).astype(F32)
         part = jnp.sum(act * raw, axis=1, keepdims=True)
         score = part if score is None else score + part
-        grad_act = gate * raw
-        grad_gate = grad_act * up_pre * sigma * (1.0 + gate_pre * (1.0 - sigma))
-        grad_ref[:, n : n + step] = grad_gate.astype(BF16)
-        grad_ref[:, hidden + n : hidden + n + step] = (grad_act * swish).astype(BF16)
+        slope = sigma + swish * (1.0 - sigma)
+        grad_ref[:, n : n + step] = (raw * up_pre * slope).astype(BF16)
+        grad_ref[:, hidden + n : hidden + n + step] = (raw * swish).astype(BF16)
     score_ref[...] = jnp.broadcast_to(score, score_ref.shape)
 
 
@@ -191,9 +196,9 @@
     return pl.pallas_call(
         functools.partial(dispatch_kernel, cap),
         out_shape=[
-            pltpu.VMEM((rows, width + LANES), BF16),
-            pltpu.VMEM((rows, tokens), BF16),
-            pltpu.VMEM((rows, tokens), BF16),
+            pltpu.VMEM((rows, width), BF16),
+            pltpu.VMEM((rows, tokens), F32),
+            pltpu.VMEM((rows, tokens), F32),
         ],
         in_specs=[whole(pltpu.HBM)] * 3,
         out_specs=[whole()] * 3,
@@ -201,7 +206,7 @@
             pltpu.VMEM(routes.shape, routes.dtype),
             pltpu.VMEM(gates.shape, gates.dtype),
             pltpu.VMEM(grad.shape, grad.dtype),
-            pltpu.VMEM((blocks, tokens, block), F32),
+            pltpu.VMEM((blocks, tokens, block), BF16),
             pltpu.SemaphoreType.DMA((3,)),
         ],
         compiler_params=pltpu.CompilerParams(vmem_limit_bytes=16 << 20),
@@ -230,7 +235,7 @@
             pl.BlockSpec((tile, pre.shape[1]), lambda i: (i, 0)),
             pl.BlockSpec((tile, LANES), lambda i: (i, 0)),
         ],
-        scratch_shapes=[pltpu.VMEM((blocks, tile, block), F32)],
+        scratch_shapes=[pltpu.VMEM((blocks, tile, block), BF16)],
         compiler_params=pltpu.CompilerParams(vmem_limit_bytes=26 << 20),
         cost_estimate=SMALL,
         name="gradients",
@@ -270,31 +275,21 @@
 SMALL = pl.CostEstimate(flops=1 << 10, bytes_accessed=1 << 10, transcendentals=0)
 
 
-def first_terms(rows, pre, block):
-    hidden = pre.shape[1] // 2
-    return pl.pallas_call(
-        first_terms_kernel,
-        out_shape=[pltpu.VMEM((rows.shape[0], hidden), BF16)]
-        + [pltpu.VMEM((2, block, hidden), BF16)] * 2,
+def terms(kernel, name, counts, rows, other, block, act=None):
+    hidden = (other if act is None else act).shape[1]
+    if act is None:
+        hidden = hidden // 2
+    first = [pltpu.VMEM((rows.shape[0], hidden), BF16)] if act is None else []
+    outs = first + [pltpu.VMEM((count, block, hidden), BF16) for count in counts]
+    return pl.pallas_call(
+        kernel,
+        out_shape=outs,
         in_specs=[whole()] * 2,
-        out_specs=[whole()] * 3,
+        out_specs=[whole()] * len(outs),
         compiler_params=pltpu.CompilerParams(vmem_limit_bytes=LIMIT),
         cost_estimate=SMALL,
-        name="first_terms",
-    )(rows, pre)
-
-
-def more_terms(rows, weighted, first, last, block):
-    hidden = weighted.shape[1]
-    return pl.pallas_call(
-        functools.partial(more_terms_kernel, first, last),
-        out_shape=[pltpu.VMEM((last - first, block, hidden), BF16)] * 2,
-        in_specs=[whole()] * 2,
-        out_specs=[whole()] * 2,
-        compiler_params=pltpu.CompilerParams(vmem_limit_bytes=LIMIT),
-        cost_estimate=SMALL,
-        name="more_terms",
-    )(rows, weighted)
+        name=name,
+    )(rows, other if act is None else act)
 
 
 def open_sums(mine, theirs):
@@ -349,7 +344,7 @@
         )
         return moved.reshape(rows_in, x.shape[1])
 
-    send, hot0, hot1 = dispatch(
+    send, inverse0, inverse1 = dispatch(
         *[
             pltpu.with_memory_space_constraint(x, pltpu.HBM)
             for x in (routes.T, gates.T, out_grad)
@@ -366,31 +361,38 @@
         pltpu.with_memory_space_constraint(x, pltpu.VMEM)
         for x in (arrived, pre_block, down_weight[0])
     ]
-    weighted, theirs_e, mine_e = first_terms(arrived, pre_block, rows)
+    act, theirs_e = terms(first_terms_kernel, "first_terms", [2], arrived, pre_block, rows)
     theirs_e = swap(theirs_e, n_ed)
-    theirs, mine = more_terms(arrived, weighted, 2, n_ed // 2, rows)
-    theirs_e, theirs, mine = tie(theirs_e, theirs, mine)
+    mine_e, theirs_f, mine_f = terms(
+        second_terms_kernel, "second_terms", [2, 2, 2], arrived, None, rows, act
+    )
+    theirs_e, mine_e, theirs_f, mine_f = tie(theirs_e, mine_e, theirs_f, mine_f)
     even, odd = open_sums(mine_e, theirs_e)
-    even, odd, theirs, arrived = tie(even, odd, theirs, arrived)
+    even, odd, theirs_f, arrived, act = tie(even, odd, theirs_f, arrived, act)
     even, odd = hop(even, n_ed), hop(odd, n_ed)
+    theirs_f = swap(theirs_f, n_ed)
+    theirs, mine = terms(
+        functools.partial(last_terms_kernel, 4), "last_terms", [4, 4], arrived, None, rows, act
+    )
+    theirs, mine, arrived = tie(theirs, mine, arrived)
     theirs = swap(theirs, n_ed)
     pre_grad, score = gradients(arrived, pre_block, weight, n_ed)
-    even, theirs, mine, score = tie(even, theirs, mine, score)
-
-    even = hop(add(0, mine, theirs, even), n_ed)
-    odd = add(1, mine, theirs, odd)
+    even, theirs_f, mine, score = tie(even, theirs_f, mine, score)
+
+    even = hop(add(0, mine_f, theirs_f, even), n_ed)
+    odd = add(1, mine_f, theirs_f, odd)
     odd, score = tie(odd, score)
     odd = hop(odd, n_ed)
     returned = exchange(score)
-    even, returned = tie(even, returned)
-
-    even = hop(add(2, mine, theirs, even), n_ed)
-    odd = hop(add(3, mine, theirs, odd), n_ed, 1)
+    even, returned, theirs = tie(even, returned, theirs)
+
+    even = hop(add(0, mine, theirs, even), n_ed)
+    odd = hop(add(1, mine, theirs, odd), n_ed, 1)
     gate_grad = jnp.stack(
-        [jnp.sum(hot0.astype(F32) * returned, axis=0), jnp.sum(hot1.astype(F32) * returned, axis=0)]
+        [jnp.sum(inverse0 * returned, axis=0), jnp.sum(inverse1 * returned, axis=0)]
     ).T
     even, gate_grad = tie(even, gate_grad)
-    even = hop(add(4, mine, theirs, even), n_ed)
+    even = hop(add(2, mine, theirs, even), n_ed)
 
     summed, note = finish(history[0], mine, theirs, even, odd, n_ed)
     notes = lax.all_to_all(note, "ed", split_axis=0, concat_axis=0, tiled=True)

time: 128 us -> 127 us (level)
  blocking collectives: 78.4 us -> 76.8 us
    all_to_all x2, blocking collectives: 64.3 us -> 62.7 us  [exchange(): lax.all_to_all(x.reshape(n_ep, cap, x.shape[1]), 'ep', split_axis=0, conc...]
    ppermute x2 -> x3, starting transfers between devices: 2.28 us -> 2.67 us  [swap(): return lax.ppermute(x, 'ed', [(i, i ^ 1) for i in range(size)])]
    pallas_call x2 -> x3, Pallas kernels: 5.22 us -> 4.93 us  [terms(): pl.pallas_call(kernel, out_shape=outs, in_specs=[whole()] * 2, out_specs=...]
  transfers between devices with their start and end apart: 9 -> 10, of which waited for: 4 -> 5; matrix products, arithmetic and copies ran while one was open for 1% -> 1% of each run, Pallas kernels for 9% -> 8%
where the time goes in v3:
time: 127 us
  blocking collectives  76.8 us (60%)
  Pallas kernels  17.9 us (14%)
  starting transfers between devices  17 us (13%)
  waiting for transfers between devices  13.9 us (11%)
    all_to_all x2, blocking collectives, exchange(): lax.all_to_all(x.reshape(n_ep, cap, x.shape[1]), 'ep', split_axis=0, conc...  62.7 us
    ppermute x7, starting transfers between devices, hop(): lax.ppermute(x, 'ed', [(i, (i + 2 - 4 * (i % 2)) % size ^ cross) for i in...  14.4 us
    all_to_all x1, blocking collectives, body(): notes = lax.all_to_all(note, 'ed', split_axis=0, concat_axis=0, tiled=True)  14.1 us
    ppermute x7, waiting for transfers between devices, hop(): lax.ppermute(x, 'ed', [(i, (i + 2 - 4 * (i % 2)) % size ^ cross) for i in...  13.4 us
    pallas_call x1, Pallas kernels, gradients(): pl.pallas_call(raw_kernel, grid=(count // tile,), out_shape=[jax.ShapeDty...  7.69 us
    pallas_call x3, Pallas kernels, terms(): pl.pallas_call(kernel, out_shape=outs, in_specs=[whole()] * 2, out_specs=...  4.93 us
    pallas_call x1, Pallas kernels, dispatch(): pl.pallas_call(functools.partial(dispatch_kernel, cap), out_shape=[pltpu....  2.87 us
    ppermute x3, starting transfers between devices, swap(): return lax.ppermute(x, 'ed', [(i, i ^ 1) for i in range(size)])  2.67 us
  transfers between devices with their start and end apart: 10, of which 5 were waited for; matrix products, arithmetic and copies ran while one was open for 1% of the time, Pallas kernels for 8%

profile of v3, /device:TPU:1, one launch (start us, length us, event | category | flops | bytes accessed | tf_op | source)
XLA Modules:
  0.0 127.0 jit_solution(10707221425507001721)
XLA Ops:
  0.6 2.9 %dispatch.1 = (bf16[512,3584]{1,0:T(8,128)(2,1)S(1)}, f32[512,128]{1,0:T(8,128)S(1)}, f32[512,128]{1,0:T(8,128)S(1)}) custom-call(s32[2,128]{1,0:T(2,128)} %bitcast.36, bf16[2,128]{1,0:T(2,128)(2,1)} %bitcast.37, bf16[128,3584]{1,0:T(8,128)(2,1)} %grad_any.1), custom_call_target="tpu_custom_call" | custom-call | tf_op jit(solution)/shard_map/dispatch/pallas_call | solution.py:196
  3.5 0.0 copy-start
  3.5 51.7 %all_to_all.21 = bf16[16,32,3584]{2,1,0:T(8,128)(2,1)S(1)} all-to-all(bf16[16,32,3584]{2,1,0:T(8,128)(2,1)S(1)} %bitcast.28), channel_id=1, replica_groups=mesh['ed'=16,'ep'=16] {'ep'}, dimensions={0} | all-to-all | bytes 7340032 | tf_op jit(solution)/shard_map/all_to_all | solution.py:342
  55.3 0.0 copy-done
  55.3 0.0 slice-start
  55.3 1.2 first_terms.1
  56.5 2.1 %collective-permute-start = (bf16[2,224,1024]{2,1,0:T(8,128)(2,1)S(1)}, bf16[2,224,1024]{2,1,0:T(8,128)(2,1)S(1)}, u32[]{:S(2)}, u32[]{:S(2)}) collective-permute-start(bf16[2,224,1024]{2,1,0:T(8,128)(2,1)S(1)} %get-tuple-element.52), channel_id=1, source_target_pairs={{0,16},{16,0},{32,48},{48,32},{64,80},{80,64},{96,112},{112,96},{1... | collective-permute-start | bytes 2752520 | tf_op jit(solution)/shard_map/ppermute | solution.py:324
  58.6 0.0 slice-start.1
  58.6 1.6 %second_terms.1 = (bf16[2,224,1024]{2,1,0:T(8,128)(2,1)S(1)}, bf16[2,224,1024]{2,1,0:T(8,128)(2,1)S(1)}, bf16[2,224,1024]{2,1,0:T(8,128)(2,1)S(1)}) custom-call(bf16[512,3584]{1,0:T(8,128)(2,1)S(1)} %bitcast.20, bf16[512,1024]{1,0:T(8,128)(2,1)S(1)} %get-tuple-element.63.act_ref), custom_call_target="tpu_custom_call" | custom-call | flops 1024 | bytes 1024 | tf_op jit(solution)/shard_map/second_terms/pallas_call | solution.py:284
  60.2 0.5 collective-permute-done.theirs_ref
  60.7 0.2 open_sums.1
  60.9 2.1 %last_terms.1 = (bf16[4,224,1024]{2,1,0:T(8,128)(2,1)S(1)}, bf16[4,224,1024]{2,1,0:T(8,128)(2,1)S(1)}) custom-call(bf16[512,3584]{1,0:T(8,128)(2,1)S(1)} %bitcast.21, bf16[512,1024]{1,0:T(8,128)(2,1)S(1)} %get-tuple-element.63.act_ref), custom_call_target="tpu_custom_call" | custom-call | flops 1024 | bytes 1024 | tf_op jit(solution)/shard_map/last_terms/pallas_call | solution.py:284
  63.0 0.5 collective-permute-start.5
  63.4 0.1 collective-permute-start.2
  63.6 5.6 %collective-permute-start.1 = (bf16[224,1024]{1,0:T(8,128)(2,1)S(1)}, bf16[224,1024]{1,0:T(8,128)(2,1)S(1)}, u32[]{:S(2)}, u32[]{:S(2)}) collective-permute-start(bf16[224,1024]{1,0:T(8,128)(2,1)S(1)} %get-tuple-element.70), channel_id=1, source_target_pairs={{0,32},{16,240},{32,64},{48,16},{64,96},{80,48},{96,128},{112,80},... | collective-permute-start | bytes 1376264 | tf_op jit(solution)/shard_map/ppermute | solution.py:328
  69.1 0.7 collective-permute-start.4
  69.9 0.0 slice-done
  69.9 0.0 slice-done.1
  69.9 7.7 %gradients.1 = (bf16[512,2048]{1,0:T(8,128)(2,1)}, f32[512,128]{1,0:T(8,128)S(1)}) custom-call(bf16[512,3584]{1,0:T(8,128)(2,1)S(1)} %bitcast.22, bf16[512,2048]{1,0:T(8,128)(2,1)S(1)} %bitcast.24, bf16[1024,3584]{1,0:T(8,128)(2,1)S(1)} %bitcast.27), custom_call_target="tpu_custom_call" | custom-call | flops 1024 | bytes 1024 | tf_op jit(solution)/shard_map/gradients/pallas_call | solution.py:222
  77.6 0.0 collective-permute-done.1.moved_ref
  77.6 0.0 collective-permute-done.2.theirs_ref
  77.6 0.2 add.5
  77.7 0.8 collective-permute-start.3
  78.5 0.9 collective-permute-done.4.moved_ref
  79.5 0.2 add.6
  79.6 3.2 %collective-permute-start.8 = (bf16[224,1024]{1,0:T(8,128)(2,1)S(1)}, bf16[224,1024]{1,0:T(8,128)(2,1)S(1)}, u32[]{:S(2)}, u32[]{:S(2)}) collective-permute-start(bf16[224,1024]{1,0:T(8,128)(2,1)S(1)} %add.6), channel_id=1, source_target_pairs={{0,32},{16,240},{32,64},{48,16},{64,96},{80,48},{96,128},{112,80},... | collective-permute-start | bytes 1376264 | tf_op jit(solution)/shard_map/ppermute | solution.py:328
  82.8 10.9 %all_to_all.22 = f32[16,32,128]{2,1,0:T(8,128)S(1)} all-to-all(f32[16,32,128]{2,1,0:T(8,128)S(1)} %bitcast.29), channel_id=1, replica_groups=mesh['ed'=16,'ep'=16] {'ep'}, dimensions={0} | all-to-all | bytes 524288 | tf_op jit(solution)/shard_map/all_to_all | solution.py:342
  93.8 0.0 collective-permute-done.3.moved_ref
  93.8 0.0 collective-permute-done.5.theirs_ref
  93.8 0.2 add.7
  94.0 0.1 collective-permute-start.6
  94.1 0.0 collective-permute-done.8.moved_ref
  94.1 0.2 add.9
  94.2 3.0 %collective-permute-start.9 = (bf16[224,1024]{1,0:T(8,128)(2,1)S(1)}, bf16[224,1024]{1,0:T(8,128)(2,1)S(1)}, u32[]{:S(2)}, u32[]{:S(2)}) collective-permute-start(bf16[224,1024]{1,0:T(8,128)(2,1)S(1)} %add.9), channel_id=1, source_target_pairs={{0,48},{16,224},{32,80},{48,0},{64,112},{80,32},{96,144},{112,64},... | collective-permute-start | bytes 1376264 | tf_op jit(solution)/shard_map/ppermute | solution.py:328
  97.2 0.1 multiply_reduce_fusion.1
  97.3 0.6 maximum_bitcast_fusion
  97.9 0.0 copy-start.1
  97.9 3.8 %collective-permute-done.6.moved_ref = bf16[224,1024]{1,0:T(8,128)(2,1)S(1)} collective-permute-done((bf16[224,1024]{1,0:T(8,128)(2,1)S(1)}, bf16[224,1024]{1,0:T(8,128)(2,1)S(1)}, u32[]{:S(2)}, u32[]{:S(2)}) %collective-permute-start.6) | collective-permute-done | bytes 458784 | tf_op jit(solution)/shard_map/ppermute | solution.py:328
  101.7 0.2 add.8
  101.8 1.0 collective-permute-start.7
  102.8 5.2 %collective-permute-done.9.left_ref = bf16[224,1024]{1,0:T(8,128)(2,1)S(1)} collective-permute-done((bf16[224,1024]{1,0:T(8,128)(2,1)S(1)}, bf16[224,1024]{1,0:T(8,128)(2,1)S(1)}, u32[]{:S(2)}, u32[]{:S(2)}) %collective-permute-start.9) | collective-permute-done | bytes 458784 | tf_op jit(solution)/shard_map/ppermute | solution.py:328
  108.0 3.5 %collective-permute-done.7.right_ref = bf16[224,1024]{1,0:T(8,128)(2,1)S(1)} collective-permute-done((bf16[224,1024]{1,0:T(8,128)(2,1)S(1)}, bf16[224,1024]{1,0:T(8,128)(2,1)S(1)}, u32[]{:S(2)}, u32[]{:S(2)}) %collective-permute-start.7) | collective-permute-done | bytes 458784 | tf_op jit(solution)/shard_map/ppermute | solution.py:328
  111.5 0.0 copy-done.1
  111.5 0.3 finish.1
  111.8 14.1 %all_to_all.23 = f32[16,1,128]{2,1,0:T(1,128)S(1)} all-to-all(f32[16,1,128]{2,1,0:T(1,128)S(1)} %bitcast.31), channel_id=1, replica_groups=mesh['ed'=16,'ep'=16] {'ed'}, dimensions={0} | all-to-all | bytes 16384 | tf_op jit(solution)/shard_map/all_to_all | solution.py:398
  125.9 1.1 scaled.1
  (1 shorter events, 0.0 us)
Async XLA Ops:
  3.5 51.7 %copy-start = (bf16[1,1,16,32,2048]{4,3,2,1,0:T(8,128)(2,1)S(1)}, bf16[1,1,16,32,2048]{4,3,2,1,0:T(8,128)(2,1)}, u32[]{:S(2)}) copy-start(bf16[1,1,16,32,2048]{4,3,2,1,0:T(8,128)(2,1)} %param.9) | copy-start | bytes 6291460
  55.3 14.6 %slice-start = ((s8[7340032]{0:T(1024)(128)(4,1)}), s8[3145728]{0:T(1024)(128)(4,1)S(1)}, s32[]{:S(2)}) async-start(s8[7340032]{0:T(1024)(128)(4,1)} %bitcast.25), calls=%async_computation.3 | async-start | bytes 6291456
  56.5 4.2 %collective-permute-start = (bf16[2,224,1024]{2,1,0:T(8,128)(2,1)S(1)}, bf16[2,224,1024]{2,1,0:T(8,128)(2,1)S(1)}, u32[]{:S(2)}, u32[]{:S(2)}) collective-permute-start(bf16[2,224,1024]{2,1,0:T(8,128)(2,1)S(1)} %get-tuple-element.52), channel_id=1, source_target_pairs={{0,16},{16,0},{32,48},{48,32},{64,80},{80,64},{96,112},{112,96},{1... | collective-permute-start | bytes 2752520 | tf_op jit(solution)/shard_map/ppermute | solution.py:324
  58.6 11.3 %slice-start.1 = ((s8[7340032]{0:T(1024)(128)(4,1)}), s8[4194304]{0:T(1024)(128)(4,1)S(1)}, s32[]{:S(2)}) async-start(s8[7340032]{0:T(1024)(128)(4,1)} %bitcast.25), calls=%async_computation.4 | async-start | bytes 8388608
  63.0 30.8 %collective-permute-start.5 = (bf16[4,224,1024]{2,1,0:T(8,128)(2,1)S(1)}, bf16[4,224,1024]{2,1,0:T(8,128)(2,1)S(1)}, u32[]{:S(2)}, u32[]{:S(2)}) collective-permute-start(bf16[4,224,1024]{2,1,0:T(8,128)(2,1)S(1)} %get-tuple-element.81), channel_id=1, source_target_pairs={{0,16},{16,0},{32,48},{48,32},{64,80},{80,64},{96,112},{112,96},{1... | collective-permute-start | bytes 5505032 | tf_op jit(solution)/shard_map/ppermute | solution.py:324
  63.4 14.1 %collective-permute-start.2 = (bf16[2,224,1024]{2,1,0:T(8,128)(2,1)S(1)}, bf16[2,224,1024]{2,1,0:T(8,128)(2,1)S(1)}, u32[]{:S(2)}, u32[]{:S(2)}) collective-permute-start(bf16[2,224,1024]{2,1,0:T(8,128)(2,1)S(1)} %get-tuple-element.71), channel_id=1, source_target_pairs={{0,16},{16,0},{32,48},{48,32},{64,80},{80,64},{96,112},{112,96},{1... | collective-permute-start | bytes 2752520 | tf_op jit(solution)/shard_map/ppermute | solution.py:324
  63.6 14.0 %collective-permute-start.1 = (bf16[224,1024]{1,0:T(8,128)(2,1)S(1)}, bf16[224,1024]{1,0:T(8,128)(2,1)S(1)}, u32[]{:S(2)}, u32[]{:S(2)}) collective-permute-start(bf16[224,1024]{1,0:T(8,128)(2,1)S(1)} %get-tuple-element.70), channel_id=1, source_target_pairs={{0,32},{16,240},{32,64},{48,16},{64,96},{80,48},{96,128},{112,80},... | collective-permute-start | bytes 1376264 | tf_op jit(solution)/shard_map/ppermute | solution.py:328
  69.1 10.3 %collective-permute-start.4 = (bf16[224,1024]{1,0:T(8,128)(2,1)S(1)}, bf16[224,1024]{1,0:T(8,128)(2,1)S(1)}, u32[]{:S(2)}, u32[]{:S(2)}) collective-permute-start(bf16[224,1024]{1,0:T(8,128)(2,1)S(1)} %get-tuple-element.78), channel_id=1, source_target_pairs={{0,32},{16,240},{32,64},{48,16},{64,96},{80,48},{96,128},{112,80},... | collective-permute-start | bytes 1376264 | tf_op jit(solution)/shard_map/ppermute | solution.py:328
  77.7 16.0 %collective-permute-start.3 = (bf16[224,1024]{1,0:T(8,128)(2,1)S(1)}, bf16[224,1024]{1,0:T(8,128)(2,1)S(1)}, u32[]{:S(2)}, u32[]{:S(2)}) collective-permute-start(bf16[224,1024]{1,0:T(8,128)(2,1)S(1)} %add.5), channel_id=1, source_target_pairs={{0,32},{16,240},{32,64},{48,16},{64,96},{80,48},{96,128},{112,80},... | collective-permute-start | bytes 1376264 | tf_op jit(solution)/shard_map/ppermute | solution.py:328
  79.6 14.4 %collective-permute-start.8 = (bf16[224,1024]{1,0:T(8,128)(2,1)S(1)}, bf16[224,1024]{1,0:T(8,128)(2,1)S(1)}, u32[]{:S(2)}, u32[]{:S(2)}) collective-permute-start(bf16[224,1024]{1,0:T(8,128)(2,1)S(1)} %add.6), channel_id=1, source_target_pairs={{0,32},{16,240},{32,64},{48,16},{64,96},{80,48},{96,128},{112,80},... | collective-permute-start | bytes 1376264 | tf_op jit(solution)/shard_map/ppermute | solution.py:328
  94.0 7.7 %collective-permute-start.6 = (bf16[224,1024]{1,0:T(8,128)(2,1)S(1)}, bf16[224,1024]{1,0:T(8,128)(2,1)S(1)}, u32[]{:S(2)}, u32[]{:S(2)}) collective-permute-start(bf16[224,1024]{1,0:T(8,128)(2,1)S(1)} %add.7), channel_id=1, source_target_pairs={{0,32},{16,240},{32,64},{48,16},{64,96},{80,48},{96,128},{112,80},... | collective-permute-start | bytes 1376264 | tf_op jit(solution)/shard_map/ppermute | solution.py:328
  94.2 13.8 %collective-permute-start.9 = (bf16[224,1024]{1,0:T(8,128)(2,1)S(1)}, bf16[224,1024]{1,0:T(8,128)(2,1)S(1)}, u32[]{:S(2)}, u32[]{:S(2)}) collective-permute-start(bf16[224,1024]{1,0:T(8,128)(2,1)S(1)} %add.9), channel_id=1, source_target_pairs={{0,48},{16,224},{32,80},{48,0},{64,112},{80,32},{96,144},{112,64},... | collective-permute-start | bytes 1376264 | tf_op jit(solution)/shard_map/ppermute | solution.py:328
  97.9 13.6 %copy-start.1 = (f32[1,1,16]{2,1,0:T(1,128)S(1)}, f32[1,1,16]{2,1,0:T(1,128)}, u32[]{:S(2)}) copy-start(f32[1,1,16]{2,1,0:T(1,128)} %param.11) | copy-start | bytes 196
  101.8 9.7 %collective-permute-start.7 = (bf16[224,1024]{1,0:T(8,128)(2,1)S(1)}, bf16[224,1024]{1,0:T(8,128)(2,1)S(1)}, u32[]{:S(2)}, u32[]{:S(2)}) collective-permute-start(bf16[224,1024]{1,0:T(8,128)(2,1)S(1)} %add.8), channel_id=1, source_target_pairs={{0,32},{16,240},{32,64},{48,16},{64,96},{80,48},{96,128},{112,80},... | collective-permute-start | bytes 1376264 | tf_op jit(solution)/shard_map/ppermute | solution.py:328

commit v4 on v3

--- a/solution.py
+++ b/solution.py
@@ -395,7 +395,16 @@
     even = hop(add(2, mine, theirs, even), n_ed)
 
     summed, note = finish(history[0], mine, theirs, even, odd, n_ed)
-    notes = lax.all_to_all(note, "ed", split_axis=0, concat_axis=0, tiled=True)
+    high, low = range(n_ed // 4, n_ed // 2), range(n_ed // 4)
+    listed = [2 * place + core for core in (1, 0) for place in (*high, *low)]
+    notes = lax.all_to_all(
+        note,
+        "ed",
+        split_axis=0,
+        concat_axis=0,
+        tiled=True,
+        axis_index_groups=[listed],
+    )
     wgrad, new_history = scaled(notes, summed, history.shape[2])
     return (pre_grad.reshape(pre_acts.shape), wgrad[None], new_history, gate_grad)
 

time: 127 us -> 124 us (0.976)
  blocking collectives: 76.8 us -> 73.3 us
    all_to_all x1, blocking collectives: 14.1 us -> 10.6 us  [body(): lax.all_to_all(note, 'ed', split_axis=0, concat_axis=0, tiled=True, axis_...]
where the time goes in v4:
time: 124 us
  blocking collectives  73.3 us (59%)
  Pallas kernels  17.9 us (14%)
  starting transfers between devices  17 us (14%)
  waiting for transfers between devices  13.9 us (11%)
    all_to_all x2, blocking collectives, exchange(): lax.all_to_all(x.reshape(n_ep, cap, x.shape[1]), 'ep', split_axis=0, conc...  62.7 us
    ppermute x7, starting transfers between devices, hop(): lax.ppermute(x, 'ed', [(i, (i + 2 - 4 * (i % 2)) % size ^ cross) for i in...  14.4 us
    ppermute x7, waiting for transfers between devices, hop(): lax.ppermute(x, 'ed', [(i, (i + 2 - 4 * (i % 2)) % size ^ cross) for i in...  13.4 us
    all_to_all x1, blocking collectives, body(): lax.all_to_all(note, 'ed', split_axis=0, concat_axis=0, tiled=True, axis_...  10.6 us
    pallas_call x1, Pallas kernels, gradients(): pl.pallas_call(raw_kernel, grid=(count // tile,), out_shape=[jax.ShapeDty...  7.69 us
    pallas_call x3, Pallas kernels, terms(): pl.pallas_call(kernel, out_shape=outs, in_specs=[whole()] * 2, out_specs=...  4.93 us
    pallas_call x1, Pallas kernels, dispatch(): pl.pallas_call(functools.partial(dispatch_kernel, cap), out_shape=[pltpu....  2.87 us
    ppermute x3, starting transfers between devices, swap(): return lax.ppermute(x, 'ed', [(i, i ^ 1) for i in range(size)])  2.67 us
  transfers between devices with their start and end apart: 10, of which 5 were waited for; matrix products, arithmetic and copies ran while one was open for 1% of the time, Pallas kernels for 8%

profile of v4, /device:TPU:1, one launch (start us, length us, event | category | flops | bytes accessed | tf_op | source)
XLA Modules:
  0.0 123.5 jit_solution(4718246767209666391)
XLA Ops:
  0.6 2.9 %dispatch.1 = (bf16[512,3584]{1,0:T(8,128)(2,1)S(1)}, f32[512,128]{1,0:T(8,128)S(1)}, f32[512,128]{1,0:T(8,128)S(1)}) custom-call(s32[2,128]{1,0:T(2,128)} %bitcast.36, bf16[2,128]{1,0:T(2,128)(2,1)} %bitcast.37, bf16[128,3584]{1,0:T(8,128)(2,1)} %grad_any.1), custom_call_target="tpu_custom_call" | custom-call | tf_op jit(solution)/shard_map/dispatch/pallas_call | solution.py:196
  3.5 0.0 copy-start
  3.5 51.7 %all_to_all.21 = bf16[16,32,3584]{2,1,0:T(8,128)(2,1)S(1)} all-to-all(bf16[16,32,3584]{2,1,0:T(8,128)(2,1)S(1)} %bitcast.28), channel_id=1, replica_groups=mesh['ed'=16,'ep'=16] {'ep'}, dimensions={0} | all-to-all | bytes 7340032 | tf_op jit(solution)/shard_map/all_to_all | solution.py:342
  55.3 0.0 copy-done
  55.3 0.0 slice-start
  55.3 1.2 first_terms.1
  56.5 2.1 %collective-permute-start = (bf16[2,224,1024]{2,1,0:T(8,128)(2,1)S(1)}, bf16[2,224,1024]{2,1,0:T(8,128)(2,1)S(1)}, u32[]{:S(2)}, u32[]{:S(2)}) collective-permute-start(bf16[2,224,1024]{2,1,0:T(8,128)(2,1)S(1)} %get-tuple-element.52), channel_id=1, source_target_pairs={{0,16},{16,0},{32,48},{48,32},{64,80},{80,64},{96,112},{112,96},{1... | collective-permute-start | bytes 2752520 | tf_op jit(solution)/shard_map/ppermute | solution.py:324
  58.6 0.0 slice-start.1
  58.6 1.6 %second_terms.1 = (bf16[2,224,1024]{2,1,0:T(8,128)(2,1)S(1)}, bf16[2,224,1024]{2,1,0:T(8,128)(2,1)S(1)}, bf16[2,224,1024]{2,1,0:T(8,128)(2,1)S(1)}) custom-call(bf16[512,3584]{1,0:T(8,128)(2,1)S(1)} %bitcast.20, bf16[512,1024]{1,0:T(8,128)(2,1)S(1)} %get-tuple-element.63.act_ref), custom_call_target="tpu_custom_call" | custom-call | flops 1024 | bytes 1024 | tf_op jit(solution)/shard_map/second_terms/pallas_call | solution.py:284
  60.2 0.5 collective-permute-done.theirs_ref
  60.7 0.2 open_sums.1
  60.9 2.1 %last_terms.1 = (bf16[4,224,1024]{2,1,0:T(8,128)(2,1)S(1)}, bf16[4,224,1024]{2,1,0:T(8,128)(2,1)S(1)}) custom-call(bf16[512,3584]{1,0:T(8,128)(2,1)S(1)} %bitcast.21, bf16[512,1024]{1,0:T(8,128)(2,1)S(1)} %get-tuple-element.63.act_ref), custom_call_target="tpu_custom_call" | custom-call | flops 1024 | bytes 1024 | tf_op jit(solution)/shard_map/last_terms/pallas_call | solution.py:284
  63.0 0.5 collective-permute-start.5
  63.4 0.1 collective-permute-start.2
  63.6 5.6 %collective-permute-start.1 = (bf16[224,1024]{1,0:T(8,128)(2,1)S(1)}, bf16[224,1024]{1,0:T(8,128)(2,1)S(1)}, u32[]{:S(2)}, u32[]{:S(2)}) collective-permute-start(bf16[224,1024]{1,0:T(8,128)(2,1)S(1)} %get-tuple-element.70), channel_id=1, source_target_pairs={{0,32},{16,240},{32,64},{48,16},{64,96},{80,48},{96,128},{112,80},... | collective-permute-start | bytes 1376264 | tf_op jit(solution)/shard_map/ppermute | solution.py:328
  69.1 0.7 collective-permute-start.4
  69.9 0.0 slice-done
  69.9 0.0 slice-done.1
  69.9 7.7 %gradients.1 = (bf16[512,2048]{1,0:T(8,128)(2,1)}, f32[512,128]{1,0:T(8,128)S(1)}) custom-call(bf16[512,3584]{1,0:T(8,128)(2,1)S(1)} %bitcast.22, bf16[512,2048]{1,0:T(8,128)(2,1)S(1)} %bitcast.24, bf16[1024,3584]{1,0:T(8,128)(2,1)S(1)} %bitcast.27), custom_call_target="tpu_custom_call" | custom-call | flops 1024 | bytes 1024 | tf_op jit(solution)/shard_map/gradients/pallas_call | solution.py:222
  77.6 0.0 collective-permute-done.1.moved_ref
  77.6 0.0 collective-permute-done.2.theirs_ref
  77.6 0.2 add.5
  77.7 0.8 collective-permute-start.3
  78.5 0.9 collective-permute-done.4.moved_ref
  79.5 0.2 add.6
  79.6 3.2 %collective-permute-start.8 = (bf16[224,1024]{1,0:T(8,128)(2,1)S(1)}, bf16[224,1024]{1,0:T(8,128)(2,1)S(1)}, u32[]{:S(2)}, u32[]{:S(2)}) collective-permute-start(bf16[224,1024]{1,0:T(8,128)(2,1)S(1)} %add.6), channel_id=1, source_target_pairs={{0,32},{16,240},{32,64},{48,16},{64,96},{80,48},{96,128},{112,80},... | collective-permute-start | bytes 1376264 | tf_op jit(solution)/shard_map/ppermute | solution.py:328
  82.8 10.9 %all_to_all.22 = f32[16,32,128]{2,1,0:T(8,128)S(1)} all-to-all(f32[16,32,128]{2,1,0:T(8,128)S(1)} %bitcast.29), channel_id=1, replica_groups=mesh['ed'=16,'ep'=16] {'ep'}, dimensions={0} | all-to-all | bytes 524288 | tf_op jit(solution)/shard_map/all_to_all | solution.py:342
  93.8 0.0 collective-permute-done.3.moved_ref
  93.8 0.0 collective-permute-done.5.theirs_ref
  93.8 0.2 add.7
  94.0 0.1 collective-permute-start.6
  94.1 0.0 collective-permute-done.8.moved_ref
  94.1 0.2 add.9
  94.2 3.0 %collective-permute-start.9 = (bf16[224,1024]{1,0:T(8,128)(2,1)S(1)}, bf16[224,1024]{1,0:T(8,128)(2,1)S(1)}, u32[]{:S(2)}, u32[]{:S(2)}) collective-permute-start(bf16[224,1024]{1,0:T(8,128)(2,1)S(1)} %add.9), channel_id=1, source_target_pairs={{0,48},{16,224},{32,80},{48,0},{64,112},{80,32},{96,144},{112,64},... | collective-permute-start | bytes 1376264 | tf_op jit(solution)/shard_map/ppermute | solution.py:328
  97.2 0.1 multiply_reduce_fusion.1
  97.3 0.6 maximum_bitcast_fusion
  97.9 0.0 copy-start.1
  97.9 3.8 %collective-permute-done.6.moved_ref = bf16[224,1024]{1,0:T(8,128)(2,1)S(1)} collective-permute-done((bf16[224,1024]{1,0:T(8,128)(2,1)S(1)}, bf16[224,1024]{1,0:T(8,128)(2,1)S(1)}, u32[]{:S(2)}, u32[]{:S(2)}) %collective-permute-start.6) | collective-permute-done | bytes 458784 | tf_op jit(solution)/shard_map/ppermute | solution.py:328
  101.7 0.2 add.8
  101.8 1.0 collective-permute-start.7
  102.8 5.2 %collective-permute-done.9.left_ref = bf16[224,1024]{1,0:T(8,128)(2,1)S(1)} collective-permute-done((bf16[224,1024]{1,0:T(8,128)(2,1)S(1)}, bf16[224,1024]{1,0:T(8,128)(2,1)S(1)}, u32[]{:S(2)}, u32[]{:S(2)}) %collective-permute-start.9) | collective-permute-done | bytes 458784 | tf_op jit(solution)/shard_map/ppermute | solution.py:328
  108.0 3.5 %collective-permute-done.7.right_ref = bf16[224,1024]{1,0:T(8,128)(2,1)S(1)} collective-permute-done((bf16[224,1024]{1,0:T(8,128)(2,1)S(1)}, bf16[224,1024]{1,0:T(8,128)(2,1)S(1)}, u32[]{:S(2)}, u32[]{:S(2)}) %collective-permute-start.7) | collective-permute-done | bytes 458784 | tf_op jit(solution)/shard_map/ppermute | solution.py:328
  111.5 0.0 copy-done.1
  111.5 0.3 finish.1
  111.8 10.6 %all_to_all.23 = f32[16,1,128]{2,1,0:T(1,128)S(1)} all-to-all(f32[16,1,128]{2,1,0:T(1,128)S(1)} %bitcast.31), channel_id=1, replica_groups={{144,176,208,240,16,48,80,112,128,160,192,224,0,32,64,96},{145,177,209,..., dimensions={0} | all-to-all | bytes 16384 | tf_op jit(solution)/shard_map/all_to_all | solution.py:400
  122.5 1.1 scaled.1
  (1 shorter events, 0.0 us)
Async XLA Ops:
  3.5 51.7 %copy-start = (bf16[1,1,16,32,2048]{4,3,2,1,0:T(8,128)(2,1)S(1)}, bf16[1,1,16,32,2048]{4,3,2,1,0:T(8,128)(2,1)}, u32[]{:S(2)}) copy-start(bf16[1,1,16,32,2048]{4,3,2,1,0:T(8,128)(2,1)} %param.9) | copy-start | bytes 6291460
  55.3 14.6 %slice-start = ((s8[7340032]{0:T(1024)(128)(4,1)}), s8[3145728]{0:T(1024)(128)(4,1)S(1)}, s32[]{:S(2)}) async-start(s8[7340032]{0:T(1024)(128)(4,1)} %bitcast.25), calls=%async_computation.3 | async-start | bytes 6291456
  56.5 4.2 %collective-permute-start = (bf16[2,224,1024]{2,1,0:T(8,128)(2,1)S(1)}, bf16[2,224,1024]{2,1,0:T(8,128)(2,1)S(1)}, u32[]{:S(2)}, u32[]{:S(2)}) collective-permute-start(bf16[2,224,1024]{2,1,0:T(8,128)(2,1)S(1)} %get-tuple-element.52), channel_id=1, source_target_pairs={{0,16},{16,0},{32,48},{48,32},{64,80},{80,64},{96,112},{112,96},{1... | collective-permute-start | bytes 2752520 | tf_op jit(solution)/shard_map/ppermute | solution.py:324
  58.6 11.3 %slice-start.1 = ((s8[7340032]{0:T(1024)(128)(4,1)}), s8[4194304]{0:T(1024)(128)(4,1)S(1)}, s32[]{:S(2)}) async-start(s8[7340032]{0:T(1024)(128)(4,1)} %bitcast.25), calls=%async_computation.4 | async-start | bytes 8388608
  63.0 30.8 %collective-permute-start.5 = (bf16[4,224,1024]{2,1,0:T(8,128)(2,1)S(1)}, bf16[4,224,1024]{2,1,0:T(8,128)(2,1)S(1)}, u32[]{:S(2)}, u32[]{:S(2)}) collective-permute-start(bf16[4,224,1024]{2,1,0:T(8,128)(2,1)S(1)} %get-tuple-element.81), channel_id=1, source_target_pairs={{0,16},{16,0},{32,48},{48,32},{64,80},{80,64},{96,112},{112,96},{1... | collective-permute-start | bytes 5505032 | tf_op jit(solution)/shard_map/ppermute | solution.py:324
  63.4 14.1 %collective-permute-start.2 = (bf16[2,224,1024]{2,1,0:T(8,128)(2,1)S(1)}, bf16[2,224,1024]{2,1,0:T(8,128)(2,1)S(1)}, u32[]{:S(2)}, u32[]{:S(2)}) collective-permute-start(bf16[2,224,1024]{2,1,0:T(8,128)(2,1)S(1)} %get-tuple-element.71), channel_id=1, source_target_pairs={{0,16},{16,0},{32,48},{48,32},{64,80},{80,64},{96,112},{112,96},{1... | collective-permute-start | bytes 2752520 | tf_op jit(solution)/shard_map/ppermute | solution.py:324
  63.6 14.0 %collective-permute-start.1 = (bf16[224,1024]{1,0:T(8,128)(2,1)S(1)}, bf16[224,1024]{1,0:T(8,128)(2,1)S(1)}, u32[]{:S(2)}, u32[]{:S(2)}) collective-permute-start(bf16[224,1024]{1,0:T(8,128)(2,1)S(1)} %get-tuple-element.70), channel_id=1, source_target_pairs={{0,32},{16,240},{32,64},{48,16},{64,96},{80,48},{96,128},{112,80},... | collective-permute-start | bytes 1376264 | tf_op jit(solution)/shard_map/ppermute | solution.py:328
  69.1 10.3 %collective-permute-start.4 = (bf16[224,1024]{1,0:T(8,128)(2,1)S(1)}, bf16[224,1024]{1,0:T(8,128)(2,1)S(1)}, u32[]{:S(2)}, u32[]{:S(2)}) collective-permute-start(bf16[224,1024]{1,0:T(8,128)(2,1)S(1)} %get-tuple-element.78), channel_id=1, source_target_pairs={{0,32},{16,240},{32,64},{48,16},{64,96},{80,48},{96,128},{112,80},... | collective-permute-start | bytes 1376264 | tf_op jit(solution)/shard_map/ppermute | solution.py:328
  77.7 16.0 %collective-permute-start.3 = (bf16[224,1024]{1,0:T(8,128)(2,1)S(1)}, bf16[224,1024]{1,0:T(8,128)(2,1)S(1)}, u32[]{:S(2)}, u32[]{:S(2)}) collective-permute-start(bf16[224,1024]{1,0:T(8,128)(2,1)S(1)} %add.5), channel_id=1, source_target_pairs={{0,32},{16,240},{32,64},{48,16},{64,96},{80,48},{96,128},{112,80},... | collective-permute-start | bytes 1376264 | tf_op jit(solution)/shard_map/ppermute | solution.py:328
  79.6 14.4 %collective-permute-start.8 = (bf16[224,1024]{1,0:T(8,128)(2,1)S(1)}, bf16[224,1024]{1,0:T(8,128)(2,1)S(1)}, u32[]{:S(2)}, u32[]{:S(2)}) collective-permute-start(bf16[224,1024]{1,0:T(8,128)(2,1)S(1)} %add.6), channel_id=1, source_target_pairs={{0,32},{16,240},{32,64},{48,16},{64,96},{80,48},{96,128},{112,80},... | collective-permute-start | bytes 1376264 | tf_op jit(solution)/shard_map/ppermute | solution.py:328
  94.0 7.7 %collective-permute-start.6 = (bf16[224,1024]{1,0:T(8,128)(2,1)S(1)}, bf16[224,1024]{1,0:T(8,128)(2,1)S(1)}, u32[]{:S(2)}, u32[]{:S(2)}) collective-permute-start(bf16[224,1024]{1,0:T(8,128)(2,1)S(1)} %add.7), channel_id=1, source_target_pairs={{0,32},{16,240},{32,64},{48,16},{64,96},{80,48},{96,128},{112,80},... | collective-permute-start | bytes 1376264 | tf_op jit(solution)/shard_map/ppermute | solution.py:328
  94.2 13.8 %collective-permute-start.9 = (bf16[224,1024]{1,0:T(8,128)(2,1)S(1)}, bf16[224,1024]{1,0:T(8,128)(2,1)S(1)}, u32[]{:S(2)}, u32[]{:S(2)}) collective-permute-start(bf16[224,1024]{1,0:T(8,128)(2,1)S(1)} %add.9), channel_id=1, source_target_pairs={{0,48},{16,224},{32,80},{48,0},{64,112},{80,32},{96,144},{112,64},... | collective-permute-start | bytes 1376264 | tf_op jit(solution)/shard_map/ppermute | solution.py:328
  97.9 13.6 %copy-start.1 = (f32[1,1,16]{2,1,0:T(1,128)S(1)}, f32[1,1,16]{2,1,0:T(1,128)}, u32[]{:S(2)}) copy-start(f32[1,1,16]{2,1,0:T(1,128)} %param.11) | copy-start | bytes 196
  101.8 9.7 %collective-permute-start.7 = (bf16[224,1024]{1,0:T(8,128)(2,1)S(1)}, bf16[224,1024]{1,0:T(8,128)(2,1)S(1)}, u32[]{:S(2)}, u32[]{:S(2)}) collective-permute-start(bf16[224,1024]{1,0:T(8,128)(2,1)S(1)} %add.8), channel_id=1, source_target_pairs={{0,32},{16,240},{32,64},{48,16},{64,96},{80,48},{96,128},{112,80},... | collective-permute-start | bytes 1376264 | tf_op jit(solution)/shard_map/ppermute | solution.py:328

commit v5 on v4

--- a/solution.py
+++ b/solution.py
@@ -181,7 +181,9 @@
     merged, peak = best[:, :count], best[:, count : count + 1]
     ref_amax = jnp.max(merged, axis=1, keepdims=True)
     scale = 1.0 / ref_amax
-    out_ref[...] = sum_ref[...] * scale
+    tile = out_ref.shape[0]
+    here = pl.ds(pl.multiple_of(pl.program_id(0) * tile, tile), tile)
+    out_ref[...] = sum_ref[here, :] * scale
     history_ref[...] = jnp.concatenate([merged[:, 1:], peak * scale * ref_amax], axis=1)
 
 
@@ -233,7 +235,7 @@
         ],
         out_specs=[
             pl.BlockSpec((tile, pre.shape[1]), lambda i: (i, 0)),
-            pl.BlockSpec((tile, LANES), lambda i: (i, 0)),
+            pl.BlockSpec((tile, LANES), lambda i: (count // tile - 1 - i, 0)),
         ],
         scratch_shapes=[pltpu.VMEM((blocks, tile, block), BF16)],
         compiler_params=pltpu.CompilerParams(vmem_limit_bytes=26 << 20),
@@ -260,12 +262,16 @@
 def scaled(notes, summed, count):
     return pl.pallas_call(
         scale_kernel,
+        grid=(4,),
         out_shape=[
             jax.ShapeDtypeStruct(summed.shape, F32),
             jax.ShapeDtypeStruct((1, count), F32),
         ],
         in_specs=[whole()] * 2,
-        out_specs=[whole()] * 2,
+        out_specs=[
+            pl.BlockSpec((summed.shape[0] // 4, summed.shape[1]), lambda i: (i, 0)),
+            pl.BlockSpec((1, count), lambda i: (0, 0)),
+        ],
         compiler_params=pltpu.CompilerParams(vmem_limit_bytes=16 << 20),
         name="scaled",
     )(notes, summed)
@@ -383,13 +389,25 @@
     odd = add(1, mine_f, theirs_f, odd)
     odd, score = tie(odd, score)
     odd = hop(odd, n_ed)
-    returned = exchange(score)
+    turned = [*range(n_ep // 2, n_ep), *range(n_ep // 2)]
+    returned = lax.all_to_all(
+        score.reshape(n_ep, cap, LANES),
+        "ep",
+        split_axis=0,
+        concat_axis=0,
+        tiled=True,
+        axis_index_groups=[turned],
+    ).reshape(rows_in, LANES)
     even, returned, theirs = tie(even, returned, theirs)
 
     even = hop(add(0, mine, theirs, even), n_ed)
     odd = hop(add(1, mine, theirs, odd), n_ed, 1)
     gate_grad = jnp.stack(
-        [jnp.sum(inverse0 * returned, axis=0), jnp.sum(inverse1 * returned, axis=0)]
+        [
+            jnp.sum(inverse[: rows_in // 2] * returned[rows_in // 2 :], axis=0)
+            + jnp.sum(inverse[rows_in // 2 :] * returned[: rows_in // 2], axis=0)
+            for inverse in (inverse0, inverse1)
+        ]
     ).T
     even, gate_grad = tie(even, gate_grad)
     even = hop(add(2, mine, theirs, even), n_ed)

time: 124 us -> 124 us (level)
    all_to_all x2 -> x1, blocking collectives: 62.7 us -> 51.7 us  [exchange(): lax.all_to_all(x.reshape(n_ep, cap, x.shape[1]), 'ep', split_axis=0, conc...]
    all_to_all x0 -> x1, blocking collectives: none -> 10.3 us  [body(): lax.all_to_all(score.reshape(n_ep, cap, LANES), 'ep', split_axis=0, conca...]
where the time goes in v5:
time: 124 us
  blocking collectives  72.7 us (59%)
  Pallas kernels  18.6 us (15%)
  starting transfers between devices  17 us (14%)
  waiting for transfers between devices  13.9 us (11%)
    all_to_all x1, blocking collectives, exchange(): lax.all_to_all(x.reshape(n_ep, cap, x.shape[1]), 'ep', split_axis=0, conc...  51.7 us
    ppermute x7, starting transfers between devices, hop(): lax.ppermute(x, 'ed', [(i, (i + 2 - 4 * (i % 2)) % size ^ cross) for i in...  14.4 us
    ppermute x7, waiting for transfers between devices, hop(): lax.ppermute(x, 'ed', [(i, (i + 2 - 4 * (i % 2)) % size ^ cross) for i in...  13.4 us
    all_to_all x1, blocking collectives, body(): lax.all_to_all(note, 'ed', split_axis=0, concat_axis=0, tiled=True, axis_...  10.6 us
    all_to_all x1, blocking collectives, body(): lax.all_to_all(score.reshape(n_ep, cap, LANES), 'ep', split_axis=0, conca...  10.3 us
    pallas_call x1, Pallas kernels, gradients(): pl.pallas_call(raw_kernel, grid=(count // tile,), out_shape=[jax.ShapeDty...  7.69 us
    pallas_call x3, Pallas kernels, terms(): pl.pallas_call(kernel, out_shape=outs, in_specs=[whole()] * 2, out_specs=...  4.93 us
    pallas_call x1, Pallas kernels, dispatch(): pl.pallas_call(functools.partial(dispatch_kernel, cap), out_shape=[pltpu....  2.87 us
  transfers between devices with their start and end apart: 10, of which 5 were waited for; matrix products, arithmetic and copies ran while one was open for 1% of the time, Pallas kernels for 8%

profile of v5, /device:TPU:1, one launch (start us, length us, event | category | flops | bytes accessed | tf_op | source)
XLA Modules:
  0.0 123.5 jit_solution(13056647179774645352)
XLA Ops:
  0.6 2.9 %dispatch.1 = (bf16[512,3584]{1,0:T(8,128)(2,1)S(1)}, f32[512,128]{1,0:T(8,128)S(1)}, f32[512,128]{1,0:T(8,128)S(1)}) custom-call(s32[2,128]{1,0:T(2,128)} %bitcast.36, bf16[2,128]{1,0:T(2,128)(2,1)} %bitcast.37, bf16[128,3584]{1,0:T(8,128)(2,1)} %grad_any.1), custom_call_target="tpu_custom_call" | custom-call | tf_op jit(solution)/shard_map/dispatch/pallas_call | solution.py:198
  3.5 0.0 copy-start
  3.5 51.7 %all_to_all.21 = bf16[16,32,3584]{2,1,0:T(8,128)(2,1)S(1)} all-to-all(bf16[16,32,3584]{2,1,0:T(8,128)(2,1)S(1)} %bitcast.30), channel_id=1, replica_groups=mesh['ed'=16,'ep'=16] {'ep'}, dimensions={0} | all-to-all | bytes 7340032 | tf_op jit(solution)/shard_map/all_to_all | solution.py:348
  55.3 0.0 copy-done
  55.3 0.0 slice-start
  55.3 1.2 first_terms.1
  56.5 2.1 %collective-permute-start = (bf16[2,224,1024]{2,1,0:T(8,128)(2,1)S(1)}, bf16[2,224,1024]{2,1,0:T(8,128)(2,1)S(1)}, u32[]{:S(2)}, u32[]{:S(2)}) collective-permute-start(bf16[2,224,1024]{2,1,0:T(8,128)(2,1)S(1)} %get-tuple-element.52), channel_id=1, source_target_pairs={{0,16},{16,0},{32,48},{48,32},{64,80},{80,64},{96,112},{112,96},{1... | collective-permute-start | bytes 2752520 | tf_op jit(solution)/shard_map/ppermute | solution.py:330
  58.6 0.0 slice-start.1
  58.6 1.6 %second_terms.1 = (bf16[2,224,1024]{2,1,0:T(8,128)(2,1)S(1)}, bf16[2,224,1024]{2,1,0:T(8,128)(2,1)S(1)}, bf16[2,224,1024]{2,1,0:T(8,128)(2,1)S(1)}) custom-call(bf16[512,3584]{1,0:T(8,128)(2,1)S(1)} %bitcast.22, bf16[512,1024]{1,0:T(8,128)(2,1)S(1)} %get-tuple-element.63.act_ref), custom_call_target="tpu_custom_call" | custom-call | flops 1024 | bytes 1024 | tf_op jit(solution)/shard_map/second_terms/pallas_call | solution.py:290
  60.2 0.5 collective-permute-done.theirs_ref
  60.7 0.2 open_sums.1
  60.9 2.1 %last_terms.1 = (bf16[4,224,1024]{2,1,0:T(8,128)(2,1)S(1)}, bf16[4,224,1024]{2,1,0:T(8,128)(2,1)S(1)}) custom-call(bf16[512,3584]{1,0:T(8,128)(2,1)S(1)} %bitcast.23, bf16[512,1024]{1,0:T(8,128)(2,1)S(1)} %get-tuple-element.63.act_ref), custom_call_target="tpu_custom_call" | custom-call | flops 1024 | bytes 1024 | tf_op jit(solution)/shard_map/last_terms/pallas_call | solution.py:290
  63.0 0.5 collective-permute-start.5
  63.4 0.1 collective-permute-start.2
  63.6 5.6 %collective-permute-start.1 = (bf16[224,1024]{1,0:T(8,128)(2,1)S(1)}, bf16[224,1024]{1,0:T(8,128)(2,1)S(1)}, u32[]{:S(2)}, u32[]{:S(2)}) collective-permute-start(bf16[224,1024]{1,0:T(8,128)(2,1)S(1)} %get-tuple-element.70), channel_id=1, source_target_pairs={{0,32},{16,240},{32,64},{48,16},{64,96},{80,48},{96,128},{112,80},... | collective-permute-start | bytes 1376264 | tf_op jit(solution)/shard_map/ppermute | solution.py:334
  69.1 0.7 collective-permute-start.4
  69.9 0.0 slice-done
  69.9 0.0 slice-done.1
  69.9 7.7 %gradients.1 = (bf16[512,2048]{1,0:T(8,128)(2,1)}, f32[512,128]{1,0:T(8,128)S(1)}) custom-call(bf16[512,3584]{1,0:T(8,128)(2,1)S(1)} %bitcast.24, bf16[512,2048]{1,0:T(8,128)(2,1)S(1)} %bitcast.26, bf16[1024,3584]{1,0:T(8,128)(2,1)S(1)} %bitcast.29), custom_call_target="tpu_custom_call" | custom-call | flops 1024 | bytes 1024 | tf_op jit(solution)/shard_map/gradients/pallas_call | solution.py:224
  77.6 0.0 collective-permute-done.1.moved_ref
  77.6 0.0 collective-permute-done.2.theirs_ref
  77.6 0.2 add.37
  77.7 0.8 collective-permute-start.3
  78.5 0.9 collective-permute-done.4.moved_ref
  79.5 0.2 add.38
  79.6 3.2 %collective-permute-start.8 = (bf16[224,1024]{1,0:T(8,128)(2,1)S(1)}, bf16[224,1024]{1,0:T(8,128)(2,1)S(1)}, u32[]{:S(2)}, u32[]{:S(2)}) collective-permute-start(bf16[224,1024]{1,0:T(8,128)(2,1)S(1)} %add.38), channel_id=1, source_target_pairs={{0,32},{16,240},{32,64},{48,16},{64,96},{80,48},{96,128},{112,80},... | collective-permute-start | bytes 1376264 | tf_op jit(solution)/shard_map/ppermute | solution.py:334
  82.8 10.3 %all_to_all.22 = f32[16,32,128]{2,1,0:T(8,128)S(1)} all-to-all(f32[16,32,128]{2,1,0:T(8,128)S(1)} %bitcast.31), channel_id=1, replica_groups={{8,9,10,11,12,13,14,15,0,1,2,3,4,5,6,7},{24,25,26,27,28,29,30,31,16,17,..., dimensions={0} | all-to-all | bytes 524288 | tf_op jit(solution)/shard_map/all_to_all | solution.py:393
  93.1 0.0 collective-permute-done.3.moved_ref
  93.1 0.0 collective-permute-done.5.theirs_ref
  93.1 0.2 add.39
  93.3 0.1 collective-permute-start.6
  93.4 0.0 collective-permute-done.8.moved_ref
  93.4 0.2 add.41
  93.6 3.0 %collective-permute-start.9 = (bf16[224,1024]{1,0:T(8,128)(2,1)S(1)}, bf16[224,1024]{1,0:T(8,128)(2,1)S(1)}, u32[]{:S(2)}, u32[]{:S(2)}) collective-permute-start(bf16[224,1024]{1,0:T(8,128)(2,1)S(1)} %add.41), channel_id=1, source_target_pairs={{0,48},{16,224},{32,80},{48,0},{64,112},{80,32},{96,144},{112,64},... | collective-permute-start | bytes 1376264 | tf_op jit(solution)/shard_map/ppermute | solution.py:334
  96.5 0.1 multiply_reduce_fusion.2
  96.6 0.6 maximum_bitcast_fusion
  97.2 0.0 copy-start.1
  97.2 3.8 %collective-permute-done.6.moved_ref = bf16[224,1024]{1,0:T(8,128)(2,1)S(1)} collective-permute-done((bf16[224,1024]{1,0:T(8,128)(2,1)S(1)}, bf16[224,1024]{1,0:T(8,128)(2,1)S(1)}, u32[]{:S(2)}, u32[]{:S(2)}) %collective-permute-start.6) | collective-permute-done | bytes 458784 | tf_op jit(solution)/shard_map/ppermute | solution.py:334
  101.0 0.2 add.40
  101.2 1.0 collective-permute-start.7
  102.2 5.2 %collective-permute-done.9.left_ref = bf16[224,1024]{1,0:T(8,128)(2,1)S(1)} collective-permute-done((bf16[224,1024]{1,0:T(8,128)(2,1)S(1)}, bf16[224,1024]{1,0:T(8,128)(2,1)S(1)}, u32[]{:S(2)}, u32[]{:S(2)}) %collective-permute-start.9) | collective-permute-done | bytes 458784 | tf_op jit(solution)/shard_map/ppermute | solution.py:334
  107.4 3.5 %collective-permute-done.7.right_ref = bf16[224,1024]{1,0:T(8,128)(2,1)S(1)} collective-permute-done((bf16[224,1024]{1,0:T(8,128)(2,1)S(1)}, bf16[224,1024]{1,0:T(8,128)(2,1)S(1)}, u32[]{:S(2)}, u32[]{:S(2)}) %collective-permute-start.7) | collective-permute-done | bytes 458784 | tf_op jit(solution)/shard_map/ppermute | solution.py:334
  110.8 0.0 copy-done.1
  110.8 0.3 finish.1
  111.1 10.6 %all_to_all.23 = f32[16,1,128]{2,1,0:T(1,128)S(1)} all-to-all(f32[16,1,128]{2,1,0:T(1,128)S(1)} %bitcast.33), channel_id=1, replica_groups={{144,176,208,240,16,48,80,112,128,160,192,224,0,32,64,96},{145,177,209,..., dimensions={0} | all-to-all | bytes 16384 | tf_op jit(solution)/shard_map/all_to_all | solution.py:418
  121.8 1.7 %scaled.1 = (f32[224,1024]{1,0:T(8,128)}, f32[1,16]{1,0:T(1,128)}) custom-call(f32[16,128]{1,0:T(8,128)S(1)} %bitcast.32, f32[224,1024]{1,0:T(8,128)S(1)} %get-tuple-element.90.sum_ref), custom_call_target="tpu_custom_call" | custom-call | tf_op jit(solution)/shard_map/scaled/pallas_call | solution.py:263
  (2 shorter events, 0.0 us)
Async XLA Ops:
  3.5 51.7 %copy-start = (bf16[1,1,16,32,2048]{4,3,2,1,0:T(8,128)(2,1)S(1)}, bf16[1,1,16,32,2048]{4,3,2,1,0:T(8,128)(2,1)}, u32[]{:S(2)}) copy-start(bf16[1,1,16,32,2048]{4,3,2,1,0:T(8,128)(2,1)} %param.9) | copy-start | bytes 6291460
  55.3 14.6 %slice-start = ((s8[7340032]{0:T(1024)(128)(4,1)}), s8[3145728]{0:T(1024)(128)(4,1)S(1)}, s32[]{:S(2)}) async-start(s8[7340032]{0:T(1024)(128)(4,1)} %bitcast.27), calls=%async_computation.3 | async-start | bytes 6291456
  56.5 4.2 %collective-permute-start = (bf16[2,224,1024]{2,1,0:T(8,128)(2,1)S(1)}, bf16[2,224,1024]{2,1,0:T(8,128)(2,1)S(1)}, u32[]{:S(2)}, u32[]{:S(2)}) collective-permute-start(bf16[2,224,1024]{2,1,0:T(8,128)(2,1)S(1)} %get-tuple-element.52), channel_id=1, source_target_pairs={{0,16},{16,0},{32,48},{48,32},{64,80},{80,64},{96,112},{112,96},{1... | collective-permute-start | bytes 2752520 | tf_op jit(solution)/shard_map/ppermute | solution.py:330
  58.6 11.3 %slice-start.1 = ((s8[7340032]{0:T(1024)(128)(4,1)}), s8[4194304]{0:T(1024)(128)(4,1)S(1)}, s32[]{:S(2)}) async-start(s8[7340032]{0:T(1024)(128)(4,1)} %bitcast.27), calls=%async_computation.4 | async-start | bytes 8388608
  63.0 30.1 %collective-permute-start.5 = (bf16[4,224,1024]{2,1,0:T(8,128)(2,1)S(1)}, bf16[4,224,1024]{2,1,0:T(8,128)(2,1)S(1)}, u32[]{:S(2)}, u32[]{:S(2)}) collective-permute-start(bf16[4,224,1024]{2,1,0:T(8,128)(2,1)S(1)} %get-tuple-element.81), channel_id=1, source_target_pairs={{0,16},{16,0},{32,48},{48,32},{64,80},{80,64},{96,112},{112,96},{1... | collective-permute-start | bytes 5505032 | tf_op jit(solution)/shard_map/ppermute | solution.py:330
  63.4 14.1 %collective-permute-start.2 = (bf16[2,224,1024]{2,1,0:T(8,128)(2,1)S(1)}, bf16[2,224,1024]{2,1,0:T(8,128)(2,1)S(1)}, u32[]{:S(2)}, u32[]{:S(2)}) collective-permute-start(bf16[2,224,1024]{2,1,0:T(8,128)(2,1)S(1)} %get-tuple-element.71), channel_id=1, source_target_pairs={{0,16},{16,0},{32,48},{48,32},{64,80},{80,64},{96,112},{112,96},{1... | collective-permute-start | bytes 2752520 | tf_op jit(solution)/shard_map/ppermute | solution.py:330
  63.6 14.0 %collective-permute-start.1 = (bf16[224,1024]{1,0:T(8,128)(2,1)S(1)}, bf16[224,1024]{1,0:T(8,128)(2,1)S(1)}, u32[]{:S(2)}, u32[]{:S(2)}) collective-permute-start(bf16[224,1024]{1,0:T(8,128)(2,1)S(1)} %get-tuple-element.70), channel_id=1, source_target_pairs={{0,32},{16,240},{32,64},{48,16},{64,96},{80,48},{96,128},{112,80},... | collective-permute-start | bytes 1376264 | tf_op jit(solution)/shard_map/ppermute | solution.py:334
  69.1 10.3 %collective-permute-start.4 = (bf16[224,1024]{1,0:T(8,128)(2,1)S(1)}, bf16[224,1024]{1,0:T(8,128)(2,1)S(1)}, u32[]{:S(2)}, u32[]{:S(2)}) collective-permute-start(bf16[224,1024]{1,0:T(8,128)(2,1)S(1)} %get-tuple-element.78), channel_id=1, source_target_pairs={{0,32},{16,240},{32,64},{48,16},{64,96},{80,48},{96,128},{112,80},... | collective-permute-start | bytes 1376264 | tf_op jit(solution)/shard_map/ppermute | solution.py:334
  77.7 15.4 %collective-permute-start.3 = (bf16[224,1024]{1,0:T(8,128)(2,1)S(1)}, bf16[224,1024]{1,0:T(8,128)(2,1)S(1)}, u32[]{:S(2)}, u32[]{:S(2)}) collective-permute-start(bf16[224,1024]{1,0:T(8,128)(2,1)S(1)} %add.37), channel_id=1, source_target_pairs={{0,32},{16,240},{32,64},{48,16},{64,96},{80,48},{96,128},{112,80},... | collective-permute-start | bytes 1376264 | tf_op jit(solution)/shard_map/ppermute | solution.py:334
  79.6 13.7 %collective-permute-start.8 = (bf16[224,1024]{1,0:T(8,128)(2,1)S(1)}, bf16[224,1024]{1,0:T(8,128)(2,1)S(1)}, u32[]{:S(2)}, u32[]{:S(2)}) collective-permute-start(bf16[224,1024]{1,0:T(8,128)(2,1)S(1)} %add.38), channel_id=1, source_target_pairs={{0,32},{16,240},{32,64},{48,16},{64,96},{80,48},{96,128},{112,80},... | collective-permute-start | bytes 1376264 | tf_op jit(solution)/shard_map/ppermute | solution.py:334
  93.3 7.7 %collective-permute-start.6 = (bf16[224,1024]{1,0:T(8,128)(2,1)S(1)}, bf16[224,1024]{1,0:T(8,128)(2,1)S(1)}, u32[]{:S(2)}, u32[]{:S(2)}) collective-permute-start(bf16[224,1024]{1,0:T(8,128)(2,1)S(1)} %add.39), channel_id=1, source_target_pairs={{0,32},{16,240},{32,64},{48,16},{64,96},{80,48},{96,128},{112,80},... | collective-permute-start | bytes 1376264 | tf_op jit(solution)/shard_map/ppermute | solution.py:334
  93.6 13.8 %collective-permute-start.9 = (bf16[224,1024]{1,0:T(8,128)(2,1)S(1)}, bf16[224,1024]{1,0:T(8,128)(2,1)S(1)}, u32[]{:S(2)}, u32[]{:S(2)}) collective-permute-start(bf16[224,1024]{1,0:T(8,128)(2,1)S(1)} %add.41), channel_id=1, source_target_pairs={{0,48},{16,224},{32,80},{48,0},{64,112},{80,32},{96,144},{112,64},... | collective-permute-start | bytes 1376264 | tf_op jit(solution)/shard_map/ppermute | solution.py:334
  97.2 13.6 %copy-start.1 = (f32[1,1,16]{2,1,0:T(1,128)S(1)}, f32[1,1,16]{2,1,0:T(1,128)}, u32[]{:S(2)}) copy-start(f32[1,1,16]{2,1,0:T(1,128)} %param.11) | copy-start | bytes 196
  101.2 9.7 %collective-permute-start.7 = (bf16[224,1024]{1,0:T(8,128)(2,1)S(1)}, bf16[224,1024]{1,0:T(8,128)(2,1)S(1)}, u32[]{:S(2)}, u32[]{:S(2)}) collective-permute-start(bf16[224,1024]{1,0:T(8,128)(2,1)S(1)} %add.40), channel_id=1, source_target_pairs={{0,32},{16,240},{32,64},{48,16},{64,96},{80,48},{96,128},{112,80},... | collective-permute-start | bytes 1376264 | tf_op jit(solution)/shard_map/ppermute | solution.py:334
